TPU v7x, 512 devices: a whole 4x8x8 slice. The times are simulated.
512 devices in a mesh: dp: 128 (over z, y, core), query: 4 (over x).
Axes of the slice: x: 4, y: 8, z: 8, core: 2. Of those that a mesh axis runs over, the one named last changes fastest.
Arguments:
- x_act: bfloat16 [65536, 8192], P('dp', 'query'), may hold values from -18 to 18
- g_out: bfloat16 [65536, 8192], P('dp', 'query'), may hold values from -6 to 6
- proj_in: bfloat16 [8192, 64], P('query'), may hold values from -0.16572815 to 0.16572815
- proj_out: bfloat16 [8192, 64], P('query'), may hold values from -0.16572815 to 0.16572815
- doc_lengths: int32 [128, 16], P('dp'), may hold values from 1 to 256, 512 in all within a row
- query_grads: bfloat16 [4096, 2048], P('dp', 'query'), may hold values from -0.09375 to 0.09375
Outputs:
- scores: float32 [2048, 2048], P('dp', 'query')
Inputs may be any that keep to these rules, and one draw needn't show every extreme that they name: `doc_lengths`: each row sums to 512, and its largest entry is exactly 256.
All inputs are finite; a program needn't handle non-finite values.
Results may differ from a plain program's by a relative error of at most 0.0088.
Values may be sent and summed in bfloat16 or wider, within the bound.
No kernel may reach another device: no remote copies, remote signals or barrier semaphores. Data moves between devices by JAX's collectives and lax.ppermute only.
A program may use at most 64 MiB of HBM per device.

v0:
```python
import jax
import jax.numpy as jnp
from jax import lax
from jax.sharding import PartitionSpec as P

highest = lax.Precision.HIGHEST


def damped_inverse(gram_matrix):
    matrix_order = gram_matrix.shape[0]
    identity = jnp.eye(matrix_order, dtype=jnp.float32)
    damping = 0.1 * jnp.trace(gram_matrix) / matrix_order + 1e-05
    cholesky_factor = jnp.linalg.cholesky(gram_matrix + damping * identity)
    inverse_root = jax.scipy.linalg.solve_triangular(cholesky_factor, identity, lower=True)
    return jnp.dot(inverse_root.T, inverse_root, precision=highest)


def outer_sum(projected):
    return jnp.dot(projected.T, projected, preferred_element_type=jnp.float32)


def document_sums(input_block, grad_block, lengths):
    total_rows = input_block.shape[0]
    slot_count = lengths.shape[0]
    low_rank = input_block.shape[1]
    finish = jnp.cumsum(lengths)
    begins = finish - lengths
    places = jnp.arange(total_rows, dtype=jnp.int32)[:, None]
    member = ((places >= begins[None, :]) & (places < finish[None, :])).astype(jnp.bfloat16)
    weighted = (member[:, :, None] * grad_block[:, None, :]).reshape(
        total_rows, slot_count * low_rank
    )
    doc_sums = jnp.einsum("tk,tb->kb", weighted, input_block, preferred_element_type=jnp.float32)
    return (
        doc_sums.reshape(slot_count, low_rank, low_rank)
        / lengths.astype(jnp.float32)[:, None, None]
    )


def local(x_act, g_out, proj_in, proj_out, doc_lengths, query_grads):
    input_part = jnp.dot(x_act, proj_in, preferred_element_type=jnp.float32)
    grad_part = jnp.dot(g_out, proj_out, preferred_element_type=jnp.float32)
    input_sum, grad_sum = lax.psum((input_part, grad_part), "query")
    input_proj = input_sum.astype(jnp.bfloat16)
    grad_proj = grad_sum.astype(jnp.bfloat16)
    gram_input, gram_grad = lax.psum((outer_sum(input_proj), outer_sum(grad_proj)), "dp")
    total_tokens = x_act.shape[0] * lax.axis_size("dp")
    inverse_input = damped_inverse(gram_input / total_tokens)
    inverse_grad = damped_inverse(gram_grad / total_tokens)
    doc_grads = document_sums(input_proj, grad_proj, doc_lengths[0])
    slot_count = doc_grads.shape[0]
    left_side = jnp.einsum("ac,dcb->dab", inverse_grad, doc_grads, precision=highest)
    conditioned = jnp.einsum("dab,be->dae", left_side, inverse_input, precision=highest)
    flat_docs = conditioned.reshape(slot_count, -1).astype(jnp.bfloat16)
    return jnp.dot(
        flat_docs,
        lax.all_gather(query_grads, "dp", axis=0, tiled=True),
        preferred_element_type=jnp.float32,
    )


def solution(mesh):
    placed = (
        P("dp", "query"),
        P("dp", "query"),
        P("query", None),
        P("query", None),
        P("dp", None),
        P("dp", "query"),
    )
    return jax.shard_map(
        local, mesh=mesh, in_specs=placed, out_specs=P("dp", "query"), check_vma=False
    )
```

profile of v0, /device:TPU:1, one launch (start us, length us, event | category | flops | bytes accessed | tf_op | source)
XLA Modules:
  0.0 566.3 jit_solution(6281851496197976194)
XLA Ops:
  6.5 0.7 all-gather.2.cloned.1.call-update
  7.3 0.9 copy-done
  8.1 1.9 fusion.21
  10.0 0.8 fusion.22
  10.8 16.9 %all-reduce.3 = (bf16[512,64]{0,1:T(8,128)(2,1)S(1)}, bf16[512,64]{0,1:T(8,128)(2,1)S(1)}) all-reduce(f32[512,64]{0,1:T(8,128)S(1)} %fusion.21, f32[512,64]{0,1:T(8,128)S(1)} %fusion.22), channel_id=1, replica_groups=mesh['dp'=128,'query'=4] {'query'}, use_global_device_ids=true, to_apply=%region_1.0 | all-reduce | flops 65536 | bytes 393216 | tf_op jit(solution)/shard_map/psum | solution.py:43
  27.7 0.1 fusion.23
  27.9 0.2 fusion.25
  28.0 497.9 %all-reduce = (f32[64,64]{0,1:T(8,128)S(1)}, f32[64,64]{0,1:T(8,128)S(1)}) all-reduce(f32[64,64]{0,1:T(8,128)S(1)} %fusion.23, f32[64,64]{0,1:T(8,128)S(1)} %fusion.25), channel_id=1, replica_groups=mesh['dp'=128,'query'=4] {'dp'}, use_global_device_ids=true, to_apply=%region_3.0 | all-reduce | flops 8192 | bytes 65536 | tf_op jit(solution)/shard_map/psum | solution.py:46
  525.9 0.6 select_reduce_fusion.3
  527.1 0.6 select_reduce_fusion.2
  528.4 0.1 copy.17
  528.5 5.8 %cholesky.55 = f32[64,64]{1,0:T(8,128)S(1)} custom-call(f32[64,64]{1,0:T(8,128)S(1)} %fusion.12), custom_call_target="Cholesky" | custom-call | tf_op jit(solution)/shard_map/jit(cholesky)/cholesky | solution.py:13
  534.4 0.6 compare_reduce_fusion
  535.0 0.7 fusion.10
  535.7 4.9 custom-call.7
  540.6 0.1 copy.15
  540.7 5.8 %cholesky.44 = f32[64,64]{1,0:T(8,128)S(1)} custom-call(f32[64,64]{1,0:T(8,128)S(1)} %fusion.14), custom_call_target="Cholesky" | custom-call | tf_op jit(solution)/shard_map/jit(cholesky)/cholesky | solution.py:13
  546.6 0.6 compare_reduce_fusion.1
  547.2 0.7 fusion.9
  547.9 4.9 custom-call.6
  552.8 0.1 copy.13
  552.9 0.1 reduce.4
  553.1 0.2 fusion.5
  553.3 0.2 convolution_bitcast_fusion.1
  553.5 0.2 fusion.7
  553.8 0.2 convolution_bitcast_fusion.2
  554.0 0.1 fusion.19
  554.1 0.4 convolution_divide_fusion
  554.5 0.6 convolution_bitcast_fusion
  555.1 0.6 convolution_convert_fusion
  555.7 0.3 convert_element_type.42
  556.0 3.5 fusion.24
  (16 shorter events, 0.2 us)
Async XLA Ops:
  6.5 1.6 copy-start
  6.5 3.5 copy-start.2
  6.5 549.5 %all-gather.2.cloned.1.call-start = ((), (), s32[]{:S(2)}) async-start(), calls=%async_computation | async-start | bytes 4227072 | tf_op jit(solution)/shard_map/all_gather | solution.py:57
  8.1 1.9 copy-start.1
  10.0 542.8 %copy-start.3 = (s32[1,16]{1,0:T(1,128)S(1)}, s32[1,16]{1,0:T(1,128)}, u32[]{:S(2)}) copy-start(s32[1,16]{1,0:T(1,128)} %param.13) | copy-start | bytes 196
Sparse Core Ops, SparseCore 0:
  10.5 90.6 all-gather.1
where the time goes:
time: 569 us; the launch traced here: 566 us
  blocking collectives  515 us (91%)
  other arithmetic  25.6 us (4%)
  between operations  14.9 us (3%)
  matrix products  8.89 us (2%)
    psum x1, blocking collectives, local(): lax.psum((outer_sum(input_proj), outer_sum(grad_proj)), 'dp')  498 us
    psum x1, blocking collectives, local(): input_sum, grad_sum = lax.psum((input_part, grad_part), 'query')  16.9 us
    another operation x6, other arithmetic, damped_inverse(): cholesky_factor = jnp.linalg.cholesky(gram_matrix + damping * identity)  13 us
  transfers between devices with their start and end apart: 1, of which 0 were waited for; matrix products, arithmetic and copies ran while one was open for 6% of the time, Pallas kernels for 0%

commit v1 on v0

--- a/solution.py
+++ b/solution.py
@@ -1,6 +1,7 @@
 import jax
 import jax.numpy as jnp
 from jax import lax
+from jax.sharding import Mesh
 from jax.sharding import PartitionSpec as P
 
 highest = lax.Precision.HIGHEST
@@ -17,6 +18,12 @@
 
 def outer_sum(projected):
     return jnp.dot(projected.T, projected, preferred_element_type=jnp.float32)
+
+
+def exchange_sum(value, axis):
+    members = lax.axis_size(axis)
+    copies = jnp.broadcast_to(value[None], (members, *value.shape))
+    return lax.all_to_all(copies, axis, 0, 0, tiled=True).sum(0)
 
 
 def document_sums(input_block, grad_block, lengths):
@@ -38,15 +45,22 @@
 
 
 def local(x_act, g_out, proj_in, proj_out, doc_lengths, query_grads):
+    rank = proj_in.shape[1]
     input_part = jnp.dot(x_act, proj_in, preferred_element_type=jnp.float32)
     grad_part = jnp.dot(g_out, proj_out, preferred_element_type=jnp.float32)
-    input_sum, grad_sum = lax.psum((input_part, grad_part), "query")
-    input_proj = input_sum.astype(jnp.bfloat16)
-    grad_proj = grad_sum.astype(jnp.bfloat16)
-    gram_input, gram_grad = lax.psum((outer_sum(input_proj), outer_sum(grad_proj)), "dp")
-    total_tokens = x_act.shape[0] * lax.axis_size("dp")
-    inverse_input = damped_inverse(gram_input / total_tokens)
-    inverse_grad = damped_inverse(gram_grad / total_tokens)
+    both_sum = exchange_sum(jnp.concatenate([input_part, grad_part], axis=1), "x")
+    both = both_sum.astype(jnp.bfloat16)
+    input_proj, grad_proj = both[:, :rank], both[:, rank:]
+    grams = jnp.concatenate([outer_sum(input_proj), outer_sum(grad_proj)], axis=1)
+    core_count = lax.axis_size("c")
+    swap = [(i, (i + 1) % core_count) for i in range(core_count)]
+    grams = grams + lax.ppermute(grams, "c", swap)
+    grams = exchange_sum(grams, "y")
+    grams = exchange_sum(grams, "z")
+    total_tokens = x_act.shape[0] * lax.axis_size(("z", "y", "c"))
+    grams = grams / total_tokens
+    inverse_input = damped_inverse(grams[:, :rank])
+    inverse_grad = damped_inverse(grams[:, rank:])
     doc_grads = document_sums(input_proj, grad_proj, doc_lengths[0])
     slot_count = doc_grads.shape[0]
     left_side = jnp.einsum("ac,dcb->dab", inverse_grad, doc_grads, precision=highest)
@@ -54,20 +68,22 @@
     flat_docs = conditioned.reshape(slot_count, -1).astype(jnp.bfloat16)
     return jnp.dot(
         flat_docs,
-        lax.all_gather(query_grads, "dp", axis=0, tiled=True),
+        lax.all_gather(query_grads, ("z", "y", "c"), axis=0, tiled=True),
         preferred_element_type=jnp.float32,
     )
 
 
 def solution(mesh):
+    split = Mesh(mesh.devices.reshape(8, 8, 2, 4), ("z", "y", "c", "x"))
+    dp = ("z", "y", "c")
     placed = (
-        P("dp", "query"),
-        P("dp", "query"),
-        P("query", None),
-        P("query", None),
-        P("dp", None),
-        P("dp", "query"),
+        P(dp, "x"),
+        P(dp, "x"),
+        P("x", None),
+        P("x", None),
+        P(dp, None),
+        P(dp, "x"),
     )
     return jax.shard_map(
-        local, mesh=mesh, in_specs=placed, out_specs=P("dp", "query"), check_vma=False
+        local, mesh=split, in_specs=placed, out_specs=P(dp, "x"), check_vma=False
     )

time: 569 us -> 116 us (0.20)
  blocking collectives: 515 us -> 15.1 us
  starting transfers between devices: 0.01 us -> 25.2 us
  waiting for transfers between devices: 0.73 us -> 21.9 us
    psum x2 -> x0, blocking collectives: 515 us -> none  [the longest x1 498 us: local(): lax.psum((outer_sum(input_proj), outer_sum(grad_proj)), 'dp')]
    all_to_all x0 -> x2, waiting for transfers between devices: none -> 20.4 us  [exchange_sum(): return lax.all_to_all(copies, axis, 0, 0, tiled=True).sum(0)]
    all_to_all x0 -> x2, starting transfers between devices: none -> 17.7 us  [exchange_sum(): return lax.all_to_all(copies, axis, 0, 0, tiled=True).sum(0)]
    all_to_all x0 -> x1, blocking collectives: none -> 15.1 us  [exchange_sum(): return lax.all_to_all(copies, axis, 0, 0, tiled=True).sum(0)]
    ppermute x0 -> x1, starting transfers between devices: none -> 7.49 us  [local(): grams = grams + lax.ppermute(grams, 'c', swap)]
  transfers between devices with their start and end apart: 1 -> 4, of which waited for: 0 -> 3; matrix products, arithmetic and copies ran while one was open for 6% -> 29% of each run, Pallas kernels for 0% -> 0%
where the time goes in v1:
time: 116 us; the launch traced here: 115 us
  other arithmetic  25.3 us (22%)
  starting transfers between devices  25.2 us (22%)
  waiting for transfers between devices  21.9 us (19%)
  blocking collectives  15.1 us (13%)
  between operations  14.9 us (13%)
  matrix products  9.71 us (8%)
  local copies, waits for them, and re-layouts  3.2 us (3%)
    all_to_all x2, waiting for transfers between devices, exchange_sum(): return lax.all_to_all(copies, axis, 0, 0, tiled=True).sum(0)  20.4 us
    all_to_all x2, starting transfers between devices, exchange_sum(): return lax.all_to_all(copies, axis, 0, 0, tiled=True).sum(0)  17.7 us
    all_to_all x1, blocking collectives, exchange_sum(): return lax.all_to_all(copies, axis, 0, 0, tiled=True).sum(0)  15.1 us
    another operation x6, other arithmetic, damped_inverse(): cholesky_factor = jnp.linalg.cholesky(gram_matrix + damping * identity)  13.1 us
    another operation x4, other arithmetic, damped_inverse(): jax.scipy.linalg.solve_triangular(cholesky_factor, identity, lower=True)  11.1 us
    ppermute x1, starting transfers between devices, local(): grams = grams + lax.ppermute(grams, 'c', swap)  7.49 us
    dot_general x1, matrix products, local(): jnp.dot(flat_docs, lax.all_gather(query_grads, ('z', 'y', 'c'), axis=0, t...  3.46 us
  transfers between devices with their start and end apart: 4, of which 3 were waited for; matrix products, arithmetic and copies ran while one was open for 29% of the time, Pallas kernels for 0%

profile of v1, /device:TPU:1, one launch (start us, length us, event | category | flops | bytes accessed | tf_op | source)
XLA Modules:
  0.0 115.3 jit_solution(2152147944059694661)
XLA Ops:
  6.5 0.7 all-gather.2.cloned.1.call-update
  7.3 0.9 copy-done
  8.1 1.9 %fusion.23 = f32[512,64]{0,1:T(8,128)S(1)} fusion(bf16[512,2048]{1,0:T(8,128)(2,1)S(1)} %copy-done, bf16[2048,64]{0,1:T(8,128)(2,1)} %param.11), kind=kOutput, calls=%fused_computation.50 | convolution fusion | flops 134217728 | bytes 2490368 | tf_op jit(solution)/shard_map/dot_general | solution.py:49
  10.0 0.8 fusion.24
  11.0 15.1 %all_to_all.15 = f32[4,512,128]{2,1,0:T(8,128)S(1)} all-to-all(f32[4,512,128]{2,1,0:T(8,128)S(1)} %broadcast_in_dim.10), channel_id=1, replica_groups=mesh['z'=8,'y'=8,'c'=2,'x'=4] {'x'}, dimensions={0} | all-to-all | bytes 2097152 | tf_op jit(solution)/shard_map/all_to_all | solution.py:26
  26.4 0.2 fusion.5
  26.7 7.5 %collective-permute-start = (f32[64,128]{1,0:T(8,128)S(1)}, f32[64,128]{1,0:T(8,128)S(1)}, u32[]{:S(2)}, u32[]{:S(2)}) collective-permute-start(f32[64,128]{1,0:T(8,128)S(1)} %pad_maximum_fusion.1), channel_id=1, source_target_pairs={{0,4},{4,0},{1,5},{5,1},{2,6},{6,2},{3,7},{7,3},{8,12},{12,8},{9,1... | collective-permute-start | bytes 98312 | tf_op jit(solution)/shard_map/ppermute | solution.py:57
  34.2 0.8 collective-permute-done
  35.1 0.7 broadcast_in_dim.11
  35.8 6.8 %all-to-all-start.1 = ((f32[8,64,128]{2,1,0:T(8,128)}), f32[8,64,128]{2,1,0:T(8,128)S(1)}, u32[]{:S(2)}, u32[]{:S(2)}) async-start(f32[8,64,128]{2,1,0:T(8,128)} %broadcast_in_dim.11), calls=%async_computation.1 | async-start | bytes 524288 | tf_op jit(solution)/shard_map/all_to_all | solution.py:26
  42.9 10.7 %all-to-all-done.1 = f32[8,64,128]{2,1,0:T(8,128)S(1)} async-done(((f32[8,64,128]{2,1,0:T(8,128)}), f32[8,64,128]{2,1,0:T(8,128)S(1)}, u32[]{:S(2)}, u32[]{:S(2)}) %all-to-all-start.1) | async-done | bytes 262176 | tf_op jit(solution)/shard_map/all_to_all | solution.py:26
  53.6 0.7 broadcast_in_dim.12
  54.3 10.9 %all-to-all-start.2 = ((f32[8,64,128]{2,1,0:T(8,128)}), f32[8,64,128]{2,1,0:T(8,128)S(1)}, u32[]{:S(2)}, u32[]{:S(2)}) async-start(f32[8,64,128]{2,1,0:T(8,128)} %broadcast_in_dim.12), calls=%async_computation.2 | async-start | bytes 524288 | tf_op jit(solution)/shard_map/all_to_all | solution.py:26
  65.3 0.4 convolution_divide_fusion
  65.7 9.6 %all-to-all-done.2 = f32[8,64,128]{2,1,0:T(8,128)S(1)} async-done(((f32[8,64,128]{2,1,0:T(8,128)}), f32[8,64,128]{2,1,0:T(8,128)S(1)}, u32[]{:S(2)}, u32[]{:S(2)}) %all-to-all-start.2) | async-done | bytes 262176 | tf_op jit(solution)/shard_map/all_to_all | solution.py:26
  75.5 0.6 select_reduce_fusion.2
  77.6 5.8 %cholesky.55 = f32[64,64]{1,0:T(8,128)S(1)} custom-call(f32[64,64]{1,0:T(8,128)S(1)} %get-tuple-element.13), custom_call_target="Cholesky" | custom-call | tf_op jit(solution)/shard_map/jit(cholesky)/cholesky | solution.py:14
  83.5 0.6 compare_reduce_fusion
  84.1 0.7 fusion.13
  84.8 4.9 %custom-call.7 = f32[1,64,64]{1,2,0:T(8,128)S(1)} custom-call(f32[1,64,64]{2,1,0:T(8,128)S(1)} %fusion.13), custom_call_target="InvertDiagBlocksLowerTriangular" | custom-call | tf_op jit(solution)/shard_map/jit(_solve_triangular)/triangular_solve | solution.py:15
  89.7 5.9 %cholesky.44 = f32[64,64]{1,0:T(8,128)S(1)} custom-call(f32[64,64]{1,0:T(8,128)S(1)} %get-tuple-element.14), custom_call_target="Cholesky" | custom-call | tf_op jit(solution)/shard_map/jit(cholesky)/cholesky | solution.py:14
  95.6 0.6 compare_reduce_fusion.1
  96.2 0.7 fusion.12
  96.9 4.9 %custom-call.6 = f32[1,64,64]{1,2,0:T(8,128)S(1)} custom-call(f32[1,64,64]{2,1,0:T(8,128)S(1)} %fusion.12), custom_call_target="InvertDiagBlocksLowerTriangular" | custom-call | tf_op jit(solution)/shard_map/jit(_solve_triangular)/triangular_solve | solution.py:15
  101.8 0.2 fusion.8
  102.0 0.2 convolution_bitcast_fusion.1
  102.3 0.2 fusion.10
  102.5 0.2 convolution_bitcast_fusion.2
  102.7 1.0 convolution_bitcast_fusion
  103.7 1.0 convolution_convert_fusion
  104.7 0.3 convert_element_type.38
  105.0 3.5 %fusion.25 = f32[16,512]{1,0:T(8,128)} fusion(bf16[16,4096]{1,0:T(8,128)(2,1)S(1)} %convert_element_type.38, bf16[4096,512]{1,0:T(8,128)(2,1)} %all-gather.2.cloned.1.call-done), kind=kOutput, calls=%fused_computation.52 | convolution fusion | flops 67108864 | bytes 4358144 | tf_op jit(solution)/shard_map/dot_general | solution.py:69
  (33 shorter events, 1.4 us)
Async XLA Ops:
  6.5 1.6 %copy-start = (bf16[512,2048]{1,0:T(8,128)(2,1)S(1)}, bf16[512,2048]{1,0:T(8,128)(2,1)}, u32[]{:S(2)}) copy-start(bf16[512,2048]{1,0:T(8,128)(2,1)} %param.9) | copy-start | bytes 6291460
  6.5 3.5 %copy-start.2 = (bf16[2048,64]{0,1:T(8,128)(2,1)S(1)}, bf16[2048,64]{0,1:T(8,128)(2,1)}, u32[]{:S(2)}) copy-start(bf16[2048,64]{0,1:T(8,128)(2,1)} %param.12) | copy-start | bytes 786436
  6.5 98.5 %all-gather.2.cloned.1.call-start = ((), (), s32[]{:S(2)}) async-start(), calls=%async_computation.3 | async-start | bytes 4227072 | tf_op jit(solution)/shard_map/all_gather | solution.py:71
  8.1 1.9 %copy-start.1 = (bf16[512,2048]{1,0:T(8,128)(2,1)S(1)}, bf16[512,2048]{1,0:T(8,128)(2,1)}, u32[]{:S(2)}) copy-start(bf16[512,2048]{1,0:T(8,128)(2,1)} %param.10) | copy-start | bytes 6291460
  11.0 31.6 %copy-start.3 = (s32[1,16]{1,0:T(1,128)S(1)}, s32[1,16]{1,0:T(1,128)}, u32[]{:S(2)}) copy-start(s32[1,16]{1,0:T(1,128)} %param.13) | copy-start | bytes 196
  26.7 8.3 %collective-permute-start = (f32[64,128]{1,0:T(8,128)S(1)}, f32[64,128]{1,0:T(8,128)S(1)}, u32[]{:S(2)}, u32[]{:S(2)}) collective-permute-start(f32[64,128]{1,0:T(8,128)S(1)} %pad_maximum_fusion.1), channel_id=1, source_target_pairs={{0,4},{4,0},{1,5},{5,1},{2,6},{6,2},{3,7},{7,3},{8,12},{12,8},{9,1... | collective-permute-start | bytes 98312 | tf_op jit(solution)/shard_map/ppermute | solution.py:57
  35.8 17.8 %all-to-all-start.1 = ((f32[8,64,128]{2,1,0:T(8,128)}), f32[8,64,128]{2,1,0:T(8,128)S(1)}, u32[]{:S(2)}, u32[]{:S(2)}) async-start(f32[8,64,128]{2,1,0:T(8,128)} %broadcast_in_dim.11), calls=%async_computation.1 | async-start | bytes 524288 | tf_op jit(solution)/shard_map/all_to_all | solution.py:26
  54.3 21.0 %all-to-all-start.2 = ((f32[8,64,128]{2,1,0:T(8,128)}), f32[8,64,128]{2,1,0:T(8,128)S(1)}, u32[]{:S(2)}, u32[]{:S(2)}) async-start(f32[8,64,128]{2,1,0:T(8,128)} %broadcast_in_dim.12), calls=%async_computation.2 | async-start | bytes 524288 | tf_op jit(solution)/shard_map/all_to_all | solution.py:26
Sparse Core Ops, SparseCore 0:
  10.5 91.4 all-gather.1

commit v2 on v0

v2 whole, which is shorter than its diff:
```python
import jax
import jax.numpy as jnp
from jax import lax
from jax.experimental import pallas as pl
from jax.experimental.pallas import tpu as pltpu
from jax.sharding import PartitionSpec as P

highest = lax.Precision.HIGHEST
f32 = jnp.float32
bf16 = jnp.bfloat16
RING = 8
CORES = 2


def place(z, y, core):
    return ((z % RING) * RING + y % RING) * CORES + core


def step_factors(lowest, steps):
    factors = []
    for _ in range(steps):
        factors.append(2.0 / (1.0 + lowest))
        gap = (1.0 - lowest) / (1.0 + lowest)
        lowest = 1.0 - gap * gap
    return factors


def damped_inverses(grams):
    n = grams.shape[0]
    lane = lax.broadcasted_iota(jnp.int32, (n, 2 * n), 1)
    blocks = jnp.concatenate(
        [jnp.where(lane < n, grams, 0.0), jnp.where(lane >= n, grams, 0.0)], axis=0
    )
    row = lax.broadcasted_iota(jnp.int32, (2 * n, 2 * n), 0)
    col = lax.broadcasted_iota(jnp.int32, (2 * n, 2 * n), 1)
    eye = (row == col).astype(f32)
    diagonal = blocks * eye
    first = jnp.sum(diagonal[:n], keepdims=True)
    second = jnp.sum(diagonal[n:], keepdims=True)
    at_row = lax.broadcasted_iota(jnp.int32, (2 * n, 1), 0)
    trace = jnp.where(at_row < n, first, second)
    damping = 0.1 * trace / n + 1e-05
    shrink = 1.0 / (trace + damping)
    matrix = (blocks + damping * eye) * shrink
    factors = step_factors(1.0 / 642.0, 8)
    head = factors[0]
    guess = (2.0 * head) * eye - (head * head) * matrix
    for factor in factors[1:]:
        product = jnp.dot(matrix, guess, precision=highest, preferred_element_type=f32)
        correction = jnp.dot(guess, product, precision=highest, preferred_element_type=f32)
        guess = (2.0 * factor) * guess - (factor * factor) * correction
    return guess * shrink


def finish(token_share, pieces_ref, own_ref, peer_ref, near_hbm, far_hbm, mine_ref, other_ref, held, by_row, arrived):
    steps = held.shape[1]
    copies = [
        [
            pltpu.make_async_copy(hbm.at[t], held.at[s, t], arrived.at[s, t])
            for t in range(steps)
        ]
        for s, hbm in enumerate((near_hbm, far_hbm))
    ]
    for side in copies:
        for copy in side:
            copy.start()
    me = lax.axis_index("dp")
    core = lax.rem(me, CORES)
    at_y = lax.rem(lax.div(me, CORES), RING)
    at_z = lax.div(me, CORES * RING)
    parity = lax.rem(jnp.where(core == 0, at_y, at_z), 2)
    grams = pieces_ref[0]
    for k in range(1, pieces_ref.shape[0]):
        grams = grams + pieces_ref[k]
    inverses = damped_inverses(grams * token_share)
    n = grams.shape[0]
    half = n // CORES
    fit = 2 * n // half
    docs = CORES * own_ref.shape[1] // n
    left = [
        jnp.dot(inverses[n:, n:], ref[...], precision=highest, preferred_element_type=f32)
        for ref in (own_ref, peer_ref)
    ]
    inverse_input = inverses[:n]
    column = lax.broadcasted_iota(jnp.int32, (n, 2 * n), 1)
    columns = jnp.where(core == 0, inverse_input, pltpu.roll(inverse_input, 2 * n - half, 1))
    columns = jnp.where(column < half, columns, 0.0)
    right = jnp.concatenate(
        [columns] + [pltpu.roll(columns, half * j, 1) for j in range(1, fit)], axis=0
    )
    groups = docs // fit
    stack = jnp.concatenate(
        [side[:, g * fit * n : (g + 1) * fit * n] for side in left for g in range(groups // CORES)],
        axis=0,
    )
    both = jnp.dot(stack, right, precision=highest, preferred_element_type=f32)
    for j in range(fit):
        turned = both if j == 0 else pltpu.roll(both, 2 * n - half * j, 1)
        for g in range(groups):
            by_row[pl.ds(g * fit + j, n, stride=docs), :] = turned[g * n : (g + 1) * n]
    lane = lax.broadcasted_iota(jnp.int32, (docs, 2 * n), 1)
    total = jnp.zeros((docs, mine_ref.shape[1]), f32)
    for s in range(2):
        odd = parity if s == 0 else 1 - parity
        for t in range(steps):
            wide = []
            for first in range(0, RING, fit):
                block = None
                for j in range(fit):
                    k = first + j
                    a = jnp.where(
                        core == 0,
                        (2 * t + k // 4) * RING + 2 * (k % 4) + odd,
                        (2 * t + odd) * RING + k,
                    )
                    rows = by_row[pl.ds(pl.multiple_of(a * docs, docs), docs), :]
                    if j == 0:
                        block = rows
                    else:
                        block = jnp.where(lane < half * j, block, pltpu.roll(rows, half * j, 1))
                wide.append(block.astype(bf16))
            copies[s][t].wait()
            part = held[s, t]
            total += jnp.dot(
                jnp.concatenate(wide, axis=1),
                part.reshape(part.shape[0] * part.shape[1], part.shape[2]),
                preferred_element_type=f32,
            )
    mine_ref[...] = total[: docs // CORES]
    other_ref[...] = total[docs // CORES :]


def scores_of(pieces, own_docs, peer_docs, near, far, token_count):
    rank = pieces.shape[1]
    docs = CORES * own_docs.shape[1] // rank
    columns = near.shape[-1]
    vmem = pl.BlockSpec(memory_space=pltpu.VMEM)
    hbm = pl.BlockSpec(memory_space=pltpu.HBM)
    out = jax.ShapeDtypeStruct((docs // CORES, columns), f32)
    shape = (near.shape[0] // RING, RING, *near.shape[1:])
    return pl.pallas_call(
        lambda *refs: finish(1.0 / token_count, *refs),
        out_shape=(out, out),
        in_specs=[vmem, vmem, vmem, hbm, hbm],
        out_specs=(vmem, vmem),
        scratch_shapes=[
            pltpu.VMEM((2, *shape), bf16),
            pltpu.VMEM((rank * docs, 2 * rank), f32),
            pltpu.SemaphoreType.DMA((2, shape[0])),
        ],
        compiler_params=pltpu.CompilerParams(vmem_limit_bytes=32 * 1024 * 1024),
        cost_estimate=pl.CostEstimate(
            flops=docs * rank * rank * columns,
            bytes_accessed=rank * rank * columns,
            transcendentals=0,
        ),
        name="finish",
    )(pieces, own_docs, peer_docs, near.reshape(shape), far.reshape(shape))


def exchange(value, axis, groups=None):
    members = len(groups[0]) if groups else lax.axis_size(axis)
    copies = jnp.broadcast_to(value[None], (members, *value.shape))
    return lax.all_to_all(copies, axis, 0, 0, axis_index_groups=groups, tiled=True)


def along_y():
    return [[place(z, y, k) for y in range(RING)] for z in range(RING) for k in range(CORES)]


def along_z():
    return [[place(z, y, k) for z in range(RING)] for y in range(RING) for k in range(CORES)]


def core_dependent():
    halves = [range(p, RING, 2) for p in range(2)]
    return [[place(z, y, 0) for z in range(RING) for y in half] for half in halves] + [
        [place(z, y, 1) for z in half for y in range(RING)] for half in halves
    ]


def from_neighbour(value):
    pairs = []
    for z in range(RING):
        for y in range(RING):
            pairs.append((place(z, y ^ 1, 0), place(z, y, 0)))
            pairs.append((place(z ^ 1, y, 1), place(z, y, 1)))
    return lax.ppermute(value, "dp", pairs)


def swap_cores(value):
    count = lax.axis_size("dp")
    return lax.ppermute(value, "dp", [(i, i ^ 1) for i in range(count)])


def outer_sum(projected):
    return jnp.dot(projected.T, projected, preferred_element_type=f32)


def document_sums(input_block, grad_block, lengths):
    total_rows, low_rank = input_block.shape
    slot_count = lengths.shape[0]
    finish_at = jnp.cumsum(lengths)
    begins = finish_at - lengths
    places = jnp.arange(total_rows, dtype=jnp.int32)[:, None]
    member = ((places >= begins[None, :]) & (places < finish_at[None, :])).astype(bf16)
    spread = (member[:, :, None] * input_block[:, None, :]).reshape(
        total_rows, slot_count * low_rank
    )
    sums = jnp.dot(grad_block.T, spread, preferred_element_type=f32)
    return sums / jnp.repeat(lengths.astype(f32), low_rank)[None, :]


def local(x_act, g_out, proj_in, proj_out, doc_lengths, query_grads):
    rank = proj_in.shape[1]
    tokens = x_act.shape[0]
    slots = doc_lengths.shape[1]
    near = exchange(query_grads, "dp", core_dependent())
    far = from_neighbour(near)
    input_part = jnp.dot(x_act, proj_in, preferred_element_type=f32)
    grad_part = jnp.dot(g_out, proj_out, preferred_element_type=f32)
    own = lax.psum(jnp.concatenate([input_part, grad_part], axis=1), "query").astype(bf16)
    lengths = jnp.zeros((16, 2 * rank), bf16).at[0, :slots].set(doc_lengths[0].astype(bf16))
    peer = swap_cores(jnp.concatenate([own, lengths], axis=0))
    peer, peer_lengths = peer[:tokens], peer[tokens, :slots].astype(jnp.int32)
    grams = jnp.concatenate(
        [
            outer_sum(own[:, :rank]) + outer_sum(peer[:, :rank]),
            outer_sum(own[:, rank:]) + outer_sum(peer[:, rank:]),
        ],
        axis=1,
    )
    grams = exchange(grams, "dp", along_y()).sum(0)
    pieces = exchange(grams, "dp", along_z())
    own_docs = document_sums(own[:, :rank], own[:, rank:], doc_lengths[0])
    peer_docs = document_sums(peer[:, :rank], peer[:, rank:], peer_lengths)
    mine, other = scores_of(
        pieces, own_docs, peer_docs, near, far, tokens * lax.axis_size("dp")
    )
    return mine + swap_cores(other)


def solution(mesh):
    placed = (
        P("dp", "query"),
        P("dp", "query"),
        P("query", None),
        P("query", None),
        P("dp", None),
        P("dp", "query"),
    )
    return jax.shard_map(
        local, mesh=mesh, in_specs=placed, out_specs=P("dp", "query"), check_vma=False
    )
```

time: 569 us -> 99.6 us (0.18)
  blocking collectives: 515 us -> 17.2 us
  starting transfers between devices: 0.01 us -> 43.7 us
  other arithmetic: 25.6 us -> 3.64 us
  between operations: 14.9 us -> 0.18 us
  waiting for transfers between devices: 0.73 us -> 14.7 us
  Pallas kernels: 0 us -> 6.66 us
  local copies, waits for them, and re-layouts: 1.41 us -> 7.54 us
    psum x2 -> x1, blocking collectives: 515 us -> 17.2 us  [local(): lax.psum(jnp.concatenate([input_part, grad_part], axis=1), 'query')]
    all_to_all x0 -> x3, starting transfers between devices: none -> 31 us  [exchange(): lax.all_to_all(copies, axis, 0, 0, axis_index_groups=groups, tiled=True)]
    another operation x12 -> x4, other arithmetic: 24.3 us -> 0.31 us  [the longest x6 13 us: damped_inverse(): cholesky_factor = jnp.linalg.cholesky(gram_matrix + damping * identity)]
    all_to_all x0 -> x3, waiting for transfers between devices: none -> 13.8 us  [exchange(): lax.all_to_all(copies, axis, 0, 0, axis_index_groups=groups, tiled=True)]
    ppermute x0 -> x3, starting transfers between devices: none -> 12.6 us  [the longest x2 9.53 us: swap_cores(): return lax.ppermute(value, 'dp', [(i, i ^ 1) for i in range(count)])]
    pallas_call x0 -> x1, Pallas kernels: none -> 6.66 us  [scores_of(): pl.pallas_call(lambda *refs: finish(1.0 / token_count, *refs), out_shape=...]
  transfers between devices with their start and end apart: 1 -> 6, of which waited for: 0 -> 3; matrix products, arithmetic and copies ran while one was open for 6% -> 10% of each run, Pallas kernels for 0% -> 0%
where the time goes in v2:
time: 99.6 us; the launch traced here: 98.9 us
  starting transfers between devices  43.7 us (44%)
  blocking collectives  17.2 us (17%)
  waiting for transfers between devices  14.7 us (15%)
  local copies, waits for them, and re-layouts  7.54 us (8%)
  Pallas kernels  6.66 us (7%)
  matrix products  5.28 us (5%)
  other arithmetic  3.64 us (4%)
    all_to_all x3, starting transfers between devices, exchange(): lax.all_to_all(copies, axis, 0, 0, axis_index_groups=groups, tiled=True)  31 us
    psum x1, blocking collectives, local(): lax.psum(jnp.concatenate([input_part, grad_part], axis=1), 'query')  17.2 us
    all_to_all x3, waiting for transfers between devices, exchange(): lax.all_to_all(copies, axis, 0, 0, axis_index_groups=groups, tiled=True)  13.8 us
    ppermute x2, starting transfers between devices, swap_cores(): return lax.ppermute(value, 'dp', [(i, i ^ 1) for i in range(count)])  9.53 us
    pallas_call x1, Pallas kernels, scores_of(): pl.pallas_call(lambda *refs: finish(1.0 / token_count, *refs), out_shape=...  6.66 us
    broadcast_in_dim x3, local copies, waits for them, and re-layouts, exchange(): copies = jnp.broadcast_to(value[None], (members, *value.shape))  3.48 us
    dot_general x2, matrix products, document_sums(): sums = jnp.dot(grad_block.T, spread, preferred_element_type=f32)  3.16 us
    ppermute x1, starting transfers between devices, from_neighbour(): return lax.ppermute(value, 'dp', pairs)  3.09 us
  transfers between devices with their start and end apart: 6, of which 3 were waited for; matrix products, arithmetic and copies ran while one was open for 10% of the time, Pallas kernels for 0%

profile of v2, /device:TPU:1, one launch (start us, length us, event | category | flops | bytes accessed | tf_op | source)
XLA Modules:
  0.0 98.9 jit_solution(9849226333568655092)
XLA Ops:
  0.0 2.0 %broadcast_in_dim.14 = bf16[32,32,512]{2,1,0:T(8,128)(2,1)} broadcast(bf16[32,512]{1,0:T(8,128)(2,1)} %param.13), dimensions={1,2} | broadcast | bytes 1081344 | tf_op jit(solution)/shard_map/broadcast_in_dim | solution.py:163
  2.0 16.5 %all-to-all-start.2 = ((bf16[32,32,512]{2,1,0:T(8,128)(2,1)}), bf16[32,32,512]{2,1,0:T(8,128)(2,1)S(1)}, u32[]{:S(2)}, u32[]{:S(2)}) async-start(bf16[32,32,512]{2,1,0:T(8,128)(2,1)} %broadcast_in_dim.14), calls=%async_computation.2 | async-start | bytes 2097152 | tf_op jit(solution)/shard_map/all_to_all | solution.py:164
  18.7 0.1 reduce.2
  18.8 0.8 fusion.17
  19.6 0.8 copy-done.3
  20.4 0.8 fusion.18
  21.2 17.2 %all-reduce.2 = bf16[512,128]{0,1:T(8,128)(2,1)S(1)} all-reduce(f32[512,128]{0,1:T(8,128)S(1)} %pad_maximum_fusion), channel_id=1, replica_groups=mesh['dp'=128,'query'=4] {'query'}, use_global_device_ids=true, to_apply=%region_0.0 | all-reduce | flops 65536 | bytes 393216 | tf_op jit(solution)/shard_map/psum | solution.py:222
  38.6 0.7 fusion.1
  39.2 5.5 %collective-permute-start = (bf16[528,128]{0,1:T(8,128)(2,1)}, bf16[528,128]{0,1:T(8,128)(2,1)S(1)}, u32[]{:S(2)}, u32[]{:S(2)}) collective-permute-start(bf16[528,128]{0,1:T(8,128)(2,1)} %fusion.1), channel_id=1, source_target_pairs={{0,4},{4,0},{8,12},{12,8},{16,20},{20,16},{24,28},{28,24},{32,36},... | collective-permute-start | bytes 405512 | tf_op jit(solution)/shard_map/ppermute | solution.py:193
  45.0 0.1 fusion.5
  45.2 1.2 %convolution_divide_fusion.1.refs_1_ = f32[64,1024]{1,0:T(8,128)} fusion(bf16[512,1024]{0,1:T(8,128)(2,1)S(1)} %bitcast.25, f32[1024]{0:T(1024)S(1)} %div.20, bf16[512,128]{0,1:T(8,128)(2,1)S(1)} %all-reduce.2), kind=kOutput, calls=%fused_computation.1 | convolution fusion | flops 67174400 | bytes 1380352 | tf_op jit(solution)/shard_map/dot_general | solution.py:210
  46.4 0.1 fusion.15
  46.8 0.1 convolution_add_fusion.1
  47.0 0.2 convolution_add_fusion
  47.2 0.7 broadcast_in_dim.10
  48.0 6.6 %all-to-all-start = ((f32[8,64,128]{2,1,0:T(8,128)}), f32[8,64,128]{2,1,0:T(8,128)S(1)}, u32[]{:S(2)}, u32[]{:S(2)}) async-start(f32[8,64,128]{2,1,0:T(8,128)} %broadcast_in_dim.10), calls=%async_computation | async-start | bytes 524288 | tf_op jit(solution)/shard_map/all_to_all | solution.py:164
  54.6 3.1 %collective-permute-start.1 = (bf16[32,32,512]{2,1,0:T(8,128)(2,1)S(1)}, bf16[32,32,512]{2,1,0:T(8,128)(2,1)}, u32[]{:S(2)}, u32[]{:S(2)}) collective-permute-start(bf16[32,32,512]{2,1,0:T(8,128)(2,1)S(1)} %all-to-all-done.2), channel_id=1, source_target_pairs={{8,0},{68,4},{0,8},{76,12},{24,16},{84,20},{16,24},{92,28},{40,32}... | collective-permute-start | bytes 3145736 | tf_op jit(solution)/shard_map/ppermute | solution.py:188
  57.7 0.7 convert_bitcast_fusion
  58.4 0.1 reduce.5
  58.5 0.8 slice.44
  59.4 0.8 fusion.11
  60.2 5.2 %all-to-all-done = f32[8,64,128]{2,1,0:T(8,128)S(1)} async-done(((f32[8,64,128]{2,1,0:T(8,128)}), f32[8,64,128]{2,1,0:T(8,128)S(1)}, u32[]{:S(2)}, u32[]{:S(2)}) %all-to-all-start) | async-done | bytes 262176 | tf_op jit(solution)/shard_map/all_to_all | solution.py:164
  65.4 0.7 broadcast_in_dim.11
  66.2 7.9 %all-to-all-start.1 = ((f32[8,64,128]{2,1,0:T(8,128)}), f32[8,64,128]{2,1,0:T(8,128)S(1)}, u32[]{:S(2)}, u32[]{:S(2)}) async-start(f32[8,64,128]{2,1,0:T(8,128)} %broadcast_in_dim.11), calls=%async_computation.1 | async-start | bytes 524288 | tf_op jit(solution)/shard_map/all_to_all | solution.py:164
  74.1 2.0 %convolution_divide_fusion.refs_2_ = f32[64,1024]{1,0:T(8,128)} fusion(bf16[512,1024]{0,1:T(8,128)(2,1)S(1)} %bitcast.24, f32[1024]{0:T(1024)S(1)} %div.23, bf16[528,128]{0,1:T(8,128)(2,1)} %copy-done.4), kind=kOutput, calls=%fused_computation | convolution fusion | flops 67174400 | bytes 1380352 | tf_op jit(solution)/shard_map/dot_general | solution.py:210
  76.1 8.6 %all-to-all-done.1.refs_0_ = f32[8,64,128]{2,1,0:T(8,128)S(1)} async-done(((f32[8,64,128]{2,1,0:T(8,128)}), f32[8,64,128]{2,1,0:T(8,128)S(1)}, u32[]{:S(2)}, u32[]{:S(2)}) %all-to-all-start.1) | async-done | bytes 262176 | tf_op jit(solution)/shard_map/all_to_all | solution.py:164
  84.8 0.9 copy-done.1
  85.7 0.9 copy-done.2
  86.7 6.7 %finish.1 = (f32[16,512]{1,0:T(8,128)S(1)}, f32[16,512]{1,0:T(8,128)S(1)}) custom-call(f32[8,64,128]{2,1,0:T(8,128)S(1)} %all-to-all-done.1.refs_0_, f32[64,1024]{1,0:T(8,128)S(1)} %copy-done.1, f32[64,1024]{1,0:T(8,128)S(1)} %copy-done.2, bf16[4,8,32,512]{3,2,1,0:T(8,128)(2,1)S(1)} %bitcast.23, bf16[4,8,32,512]{3,2,1,0:T(8,128)(2,1)} %bitcast.8.refs_4_), custom_call_target="tpu_custom_call" | custom-call | flops 67108864 | bytes 2097152 | tf_op jit(solution)/shard_map/finish/pallas_call | solution.py:141
  93.4 4.0 %collective-permute-start.2 = (f32[16,512]{1,0:T(8,128)S(1)}, f32[16,512]{1,0:T(8,128)S(1)}, u32[]{:S(2)}, u32[]{:S(2)}) collective-permute-start(f32[16,512]{1,0:T(8,128)S(1)} %get-tuple-element.20), channel_id=1, source_target_pairs={{0,4},{4,0},{8,12},{12,8},{16,20},{20,16},{24,28},{28,24},{32,36},... | collective-permute-start | bytes 98312 | tf_op jit(solution)/shard_map/ppermute | solution.py:193
  97.4 0.8 collective-permute-done.2
  98.2 0.6 add.17
  (34 shorter events, 1.1 us)
Async XLA Ops:
  0.0 18.8 %copy-start = (bf16[512,2048]{1,0:T(8,128)(2,1)S(1)}, bf16[512,2048]{1,0:T(8,128)(2,1)}, u32[]{:S(2)}) copy-start(bf16[512,2048]{1,0:T(8,128)(2,1)} %param.8) | copy-start | bytes 6291460
  0.0 18.5 %copy-start.7 = (s32[1,16]{1,0:T(1,128)S(1)}, s32[1,16]{1,0:T(1,128)}, u32[]{:S(2)}) copy-start(s32[1,16]{1,0:T(1,128)} %param.12) | copy-start | bytes 196
  0.0 18.8 %copy-start.5 = (bf16[2048,64]{0,1:T(8,128)(2,1)S(1)}, bf16[2048,64]{0,1:T(8,128)(2,1)}, u32[]{:S(2)}) copy-start(bf16[2048,64]{0,1:T(8,128)(2,1)} %param.10) | copy-start | bytes 786436
  2.0 45.2 %all-to-all-start.2 = ((bf16[32,32,512]{2,1,0:T(8,128)(2,1)}), bf16[32,32,512]{2,1,0:T(8,128)(2,1)S(1)}, u32[]{:S(2)}, u32[]{:S(2)}) async-start(bf16[32,32,512]{2,1,0:T(8,128)(2,1)} %broadcast_in_dim.14), calls=%async_computation.2 | async-start | bytes 2097152 | tf_op jit(solution)/shard_map/all_to_all | solution.py:164
  18.8 1.6 %copy-start.3 = (bf16[512,2048]{1,0:T(8,128)(2,1)S(1)}, bf16[512,2048]{1,0:T(8,128)(2,1)}, u32[]{:S(2)}) copy-start(bf16[512,2048]{1,0:T(8,128)(2,1)} %param.9) | copy-start | bytes 6291460
  18.8 1.6 %copy-start.6 = (bf16[2048,64]{0,1:T(8,128)(2,1)S(1)}, bf16[2048,64]{0,1:T(8,128)(2,1)}, u32[]{:S(2)}) copy-start(bf16[2048,64]{0,1:T(8,128)(2,1)} %param.11) | copy-start | bytes 786436
  39.2 7.3 %collective-permute-start = (bf16[528,128]{0,1:T(8,128)(2,1)}, bf16[528,128]{0,1:T(8,128)(2,1)S(1)}, u32[]{:S(2)}, u32[]{:S(2)}) collective-permute-start(bf16[528,128]{0,1:T(8,128)(2,1)} %fusion.1), channel_id=1, source_target_pairs={{0,4},{4,0},{8,12},{12,8},{16,20},{20,16},{24,28},{28,24},{32,36},... | collective-permute-start | bytes 405512 | tf_op jit(solution)/shard_map/ppermute | solution.py:193
  46.5 1.4 %copy-start.4 = (bf16[528,128]{0,1:T(8,128)(2,1)}, bf16[528,128]{0,1:T(8,128)(2,1)S(1)}, u32[]{:S(2)}) copy-start(bf16[528,128]{0,1:T(8,128)(2,1)S(1)} %collective-permute-done) | copy-start | bytes 405508
  48.0 17.5 %all-to-all-start = ((f32[8,64,128]{2,1,0:T(8,128)}), f32[8,64,128]{2,1,0:T(8,128)S(1)}, u32[]{:S(2)}, u32[]{:S(2)}) async-start(f32[8,64,128]{2,1,0:T(8,128)} %broadcast_in_dim.10), calls=%async_computation | async-start | bytes 524288 | tf_op jit(solution)/shard_map/all_to_all | solution.py:164
  54.6 30.2 %collective-permute-start.1 = (bf16[32,32,512]{2,1,0:T(8,128)(2,1)S(1)}, bf16[32,32,512]{2,1,0:T(8,128)(2,1)}, u32[]{:S(2)}, u32[]{:S(2)}) collective-permute-start(bf16[32,32,512]{2,1,0:T(8,128)(2,1)S(1)} %all-to-all-done.2), channel_id=1, source_target_pairs={{8,0},{68,4},{0,8},{76,12},{24,16},{84,20},{16,24},{92,28},{40,32}... | collective-permute-start | bytes 3145736 | tf_op jit(solution)/shard_map/ppermute | solution.py:188
  66.2 18.6 %all-to-all-start.1 = ((f32[8,64,128]{2,1,0:T(8,128)}), f32[8,64,128]{2,1,0:T(8,128)S(1)}, u32[]{:S(2)}, u32[]{:S(2)}) async-start(f32[8,64,128]{2,1,0:T(8,128)} %broadcast_in_dim.11), calls=%async_computation.1 | async-start | bytes 524288 | tf_op jit(solution)/shard_map/all_to_all | solution.py:164
  84.8 1.0 copy-start.1
  85.7 0.9 copy-start.2
  93.4 4.9 %collective-permute-start.2 = (f32[16,512]{1,0:T(8,128)S(1)}, f32[16,512]{1,0:T(8,128)S(1)}, u32[]{:S(2)}, u32[]{:S(2)}) collective-permute-start(f32[16,512]{1,0:T(8,128)S(1)} %get-tuple-element.20), channel_id=1, source_target_pairs={{0,4},{4,0},{8,12},{12,8},{16,20},{20,16},{24,28},{28,24},{32,36},... | collective-permute-start | bytes 98312 | tf_op jit(solution)/shard_map/ppermute | solution.py:193

commit v3 on v2

v3 whole, which is shorter than its diff:
```python
import jax
import jax.numpy as jnp
from jax import lax
from jax.experimental import pallas as pl
from jax.experimental.pallas import tpu as pltpu
from jax.sharding import PartitionSpec as P

highest = lax.Precision.HIGHEST
early = lax.Precision.HIGH
f32 = jnp.float32
bf16 = jnp.bfloat16
RING = 8
CORES = 2
LENGTH_ROWS = 16


def place(z, y, core):
    return ((z % RING) * RING + y % RING) * CORES + core


def step_factors(lowest, steps):
    factors = []
    for _ in range(steps):
        factors.append(2.0 / (1.0 + lowest))
        gap = (1.0 - lowest) / (1.0 + lowest)
        lowest = 1.0 - gap * gap
    return factors


def damped_inverses(blocks):
    n = blocks.shape[0] // 2
    row = lax.broadcasted_iota(jnp.int32, (2 * n, 2 * n), 0)
    col = lax.broadcasted_iota(jnp.int32, (2 * n, 2 * n), 1)
    eye = (row == col).astype(f32)
    diagonal = blocks * eye
    first = jnp.sum(diagonal[:n], keepdims=True)
    second = jnp.sum(diagonal[n:], keepdims=True)
    at_row = lax.broadcasted_iota(jnp.int32, (2 * n, 1), 0)
    trace = jnp.where(at_row < n, first, second)
    damping = 0.1 * trace / n + 1e-05
    shrink = 1.0 / (trace + damping)
    matrix = (blocks + damping * eye) * shrink
    factors = step_factors(1.0 / 642.0, 7)
    miss = eye - factors[0] * matrix
    guess = factors[0] * (eye + miss)
    for factor in factors[1:]:
        square = jnp.dot(miss, miss, precision=early, preferred_element_type=f32)
        miss = (1.0 - factor) * eye + factor * square
        product = jnp.dot(guess, miss, precision=early, preferred_element_type=f32)
        guess = factor * (guess + product)
    product = jnp.dot(matrix, guess, precision=highest, preferred_element_type=f32)
    guess = 2.0 * guess - jnp.dot(guess, product, precision=highest, preferred_element_type=f32)
    return guess * shrink


def folded_grams(own_ref, peer_ref, copies_ref):
    tokens = own_ref.shape[0] - LENGTH_ROWS
    across = (((0,), (0,)), ((), ()))
    own, peer = own_ref[:tokens], peer_ref[:tokens]
    both = lax.dot_general(own, own, across, preferred_element_type=f32) + lax.dot_general(
        peer, peer, across, preferred_element_type=f32
    )
    n = both.shape[0] // 2
    h, q = n // 2, n // 4
    lane = lax.broadcasted_iota(jnp.int32, (h, 2 * n), 1)
    top = jnp.where(lane < n, both[:h], both[n : n + h])
    low = jnp.where(lane < n, both[h:n], both[n + h :])
    low = jnp.where(lax.rem(lane[:q], n) >= h, low[:q], pltpu.roll(low[q:], 2 * n - h, 1))
    folded = jnp.concatenate([top, low], axis=0)
    for k in range(copies_ref.shape[0]):
        copies_ref[k] = folded


def unfolded(folded):
    n = folded.shape[1] // 2
    h = n // 2
    lane = lax.broadcasted_iota(jnp.int32, (h, 2 * n), 1)
    top, low = folded[:h], folded[h:]
    low = jnp.concatenate([low, pltpu.roll(low, h, 1)], axis=0)
    first, second = lane < n, lane >= n
    right = lax.rem(lane, n) >= h
    upper = jnp.concatenate(
        [
            jnp.where(first, top, 0.0),
            jnp.where(first & right, low, 0.0),
            jnp.where(second, top, 0.0),
            jnp.where(second & right, low, 0.0),
        ],
        axis=0,
    )
    none = jnp.zeros_like(top)
    corners = jnp.concatenate(
        [
            jnp.where(first & right, top, 0.0),
            none,
            jnp.where(second & right, top, 0.0),
            none,
        ],
        axis=0,
    )
    return upper + corners.T


def summed(pieces_ref):
    total = pieces_ref[0]
    for k in range(1, pieces_ref.shape[0]):
        total = total + pieces_ref[k]
    return total


def sum_and_copy(pieces_ref, copies_ref):
    total = summed(pieces_ref)
    for k in range(copies_ref.shape[0]):
        copies_ref[k] = total


def document_means(sent, slots):
    tokens = sent.shape[0] - LENGTH_ROWS
    both, lengths = sent[:tokens], sent[tokens:]
    n = both.shape[1] // 2
    wide = slots * n
    slot = lax.broadcasted_iota(jnp.int32, (2 * n, wide), 0)
    document = lax.broadcasted_iota(jnp.int32, (2 * n, wide), 1) // n
    begins = jnp.dot(
        lengths, (slot < document).astype(f32).astype(bf16), preferred_element_type=f32
    )[:1]
    length = jnp.dot(
        lengths, (slot == document).astype(f32).astype(bf16), preferred_element_type=f32
    )[:1]
    ends = begins + length
    inputs = both.astype(f32)
    lane = lax.broadcasted_iota(jnp.int32, inputs.shape, 1)
    twice = jnp.where(lane < n, inputs, pltpu.roll(inputs, n, 1))
    four = jnp.concatenate([twice, twice], axis=1)
    at = lax.broadcasted_iota(jnp.int32, four.shape, 0).astype(f32)
    means = []
    step = four.shape[1]
    for k in range(0, wide, step):
        member = (at >= begins[:, k : k + step]) & (at < ends[:, k : k + step])
        spread = jnp.where(member, four, 0.0).astype(bf16)
        sums = lax.dot_general(both, spread, (((0,), (0,)), ((), ())), preferred_element_type=f32)
        means.append(sums[n:] / length[:, k : k + step])
    return jnp.concatenate(means, axis=1)


def finish(token_share, slots, pieces_ref, own_hbm, peer_hbm, near_hbm, far_hbm, mine_ref, other_ref, held, tokens_held, by_row, arrived, tokens_arrived):
    tokens_copies = [
        pltpu.make_async_copy(hbm, tokens_held.at[s], tokens_arrived.at[s])
        for s, hbm in enumerate((own_hbm, peer_hbm))
    ]
    for copy in tokens_copies:
        copy.start()
    steps = held.shape[1]
    copies = [
        [
            pltpu.make_async_copy(hbm.at[t], held.at[s, t], arrived.at[s, t])
            for t in range(steps)
        ]
        for s, hbm in enumerate((near_hbm, far_hbm))
    ]
    for side in copies:
        for copy in side:
            copy.start()
    me = lax.axis_index("dp")
    core = lax.rem(me, CORES)
    parity = lax.rem(lax.div(me, CORES), 2)
    means = []
    for s in range(CORES):
        tokens_copies[s].wait()
        means.append(document_means(tokens_held[s], slots))
    inverses = damped_inverses(unfolded(summed(pieces_ref)) * token_share)
    n = inverses.shape[0] // 2
    half = n // CORES
    fit = 2 * n // half
    docs = CORES * slots
    left = [
        jnp.dot(inverses[n:, n:], side, precision=highest, preferred_element_type=f32)
        for side in means
    ]
    inverse_input = inverses[:n]
    column = lax.broadcasted_iota(jnp.int32, (n, 2 * n), 1)
    columns = jnp.where(core == 0, inverse_input, pltpu.roll(inverse_input, 2 * n - half, 1))
    columns = jnp.where(column < half, columns, 0.0)
    right = jnp.concatenate(
        [columns] + [pltpu.roll(columns, half * j, 1) for j in range(1, fit)], axis=0
    )
    groups = docs // fit
    stack = jnp.concatenate(
        [side[:, g * fit * n : (g + 1) * fit * n] for side in left for g in range(groups // CORES)],
        axis=0,
    )
    both = jnp.dot(stack, right, precision=highest, preferred_element_type=f32)
    for j in range(fit):
        turned = both if j == 0 else pltpu.roll(both, 2 * n - half * j, 1)
        for g in range(groups):
            by_row[pl.ds(g * fit + j, n, stride=docs), :] = turned[g * n : (g + 1) * n]
    lane = lax.broadcasted_iota(jnp.int32, (docs, 2 * n), 1)
    total = jnp.zeros((docs, mine_ref.shape[1]), f32)
    for s in range(2):
        odd = parity if s == 0 else 1 - parity
        for t in range(steps):
            wide = []
            for first in range(0, RING, fit):
                block = None
                for j in range(fit):
                    k = first + j
                    a = (2 * t + k // 4) * RING + 2 * (k % 4) + odd
                    rows = by_row[pl.ds(pl.multiple_of(a * docs, docs), docs), :]
                    if j == 0:
                        block = rows
                    else:
                        block = jnp.where(lane < half * j, block, pltpu.roll(rows, half * j, 1))
                wide.append(block.astype(bf16))
            copies[s][t].wait()
            part = held[s, t]
            total += jnp.dot(
                jnp.concatenate(wide, axis=1),
                part.reshape(part.shape[0] * part.shape[1], part.shape[2]),
                preferred_element_type=f32,
            )
    mine_ref[...] = total[: docs // CORES]
    other_ref[...] = total[docs // CORES :]


def scores_of(pieces, own, peer, near, far, slots, token_count):
    rank = own.shape[1] // 2
    docs = CORES * slots
    columns = near.shape[-1]
    vmem = pl.BlockSpec(memory_space=pltpu.VMEM)
    hbm = pl.BlockSpec(memory_space=pltpu.HBM)
    out = jax.ShapeDtypeStruct((slots, columns), f32)
    shape = (near.shape[0] // RING, RING, *near.shape[1:])
    return pl.pallas_call(
        lambda *refs: finish(1.0 / token_count, slots, *refs),
        out_shape=(out, out),
        in_specs=[vmem, hbm, hbm, hbm, hbm],
        out_specs=(vmem, vmem),
        scratch_shapes=[
            pltpu.VMEM((2, *shape), bf16),
            pltpu.VMEM((CORES, *own.shape), bf16),
            pltpu.VMEM((rank * docs, 2 * rank), f32),
            pltpu.SemaphoreType.DMA((2, shape[0])),
            pltpu.SemaphoreType.DMA((CORES,)),
        ],
        compiler_params=pltpu.CompilerParams(vmem_limit_bytes=32 * 1024 * 1024),
        cost_estimate=pl.CostEstimate(
            flops=docs * rank * rank * columns,
            bytes_accessed=rank * rank * columns,
            transcendentals=0,
        ),
        name="finish",
    )(pieces, own, peer, near.reshape(shape), far.reshape(shape))


def in_vmem(kernel, out_shape, name, *operands):
    vmem = pl.BlockSpec(memory_space=pltpu.VMEM)
    return pl.pallas_call(
        kernel,
        out_shape=jax.ShapeDtypeStruct(out_shape, f32),
        in_specs=[vmem] * len(operands),
        out_specs=vmem,
        compiler_params=pltpu.CompilerParams(vmem_limit_bytes=16 * 1024 * 1024),
        name=name,
    )(*operands)


def spread(value, members):
    return jnp.broadcast_to(value[None], (members, *value.shape))


def send(copies, groups):
    return lax.all_to_all(copies, "dp", 0, 0, axis_index_groups=groups, tiled=True)


def along_y():
    return [[place(z, y, k) for y in range(RING)] for z in range(RING) for k in range(CORES)]


def along_z():
    return [[place(z, y, k) for z in range(RING)] for y in range(RING) for k in range(CORES)]


def every_second():
    return [
        [place(z, y, k) for z in range(RING) for y in range(p, RING, 2)]
        for p in range(2)
        for k in range(CORES)
    ]


def from_neighbour(value):
    pairs = [
        (place(z, y + side, k), place(z, y, k))
        for z in range(RING)
        for y in range(RING)
        for k, side in ((0, 1), (1, -1))
    ]
    return lax.ppermute(value, "dp", pairs)


def swap_cores(value):
    count = lax.axis_size("dp")
    return lax.ppermute(value, "dp", [(i, i ^ 1) for i in range(count)])


def local(x_act, g_out, proj_in, proj_out, doc_lengths, query_grads):
    rank = proj_in.shape[1]
    tokens = x_act.shape[0]
    slots = doc_lengths.shape[1]
    groups = every_second()
    near = send(spread(query_grads, len(groups[0])), groups)
    input_part = jnp.dot(x_act, proj_in, preferred_element_type=f32)
    grad_part = jnp.dot(g_out, proj_out, preferred_element_type=f32)
    lengths = jnp.where(lax.axis_index("query") == 0, doc_lengths, 0).astype(f32)
    lengths = jnp.pad(lengths, ((0, LENGTH_ROWS - 1), (0, 2 * rank - slots)))
    parts = jnp.concatenate([jnp.concatenate([input_part, grad_part], axis=1), lengths], axis=0)
    own = lax.psum(parts, "query").astype(bf16)
    peer = swap_cores(own)
    folded = (RING, rank * 3 // 4, 2 * rank)
    copies = in_vmem(folded_grams, folded, "grams", own, peer)
    near, copies = lax.optimization_barrier((near, copies))
    copies = in_vmem(sum_and_copy, folded, "between", send(copies, along_y()))
    near, copies = lax.optimization_barrier((near, copies))
    far = from_neighbour(near)
    pieces = send(copies, along_z())
    mine, other = scores_of(
        pieces, own, peer, near, far, slots, tokens * lax.axis_size("dp")
    )
    return mine + swap_cores(other)


def solution(mesh):
    placed = (
        P("dp", "query"),
        P("dp", "query"),
        P("query", None),
        P("query", None),
        P("dp", None),
        P("dp", "query"),
    )
    return jax.shard_map(
        local, mesh=mesh, in_specs=placed, out_specs=P("dp", "query"), check_vma=False
    )
```

time: 99.6 us -> 94.3 us (0.947)
  blocking collectives: 17.2 us -> 43.3 us
  starting transfers between devices: 43.7 us -> 29.4 us
  waiting for transfers between devices: 14.7 us -> 7.85 us
  matrix products: 5.28 us -> 1.38 us
  local copies, waits for them, and re-layouts: 7.54 us -> 4.43 us
  other arithmetic: 3.64 us -> 0.76 us
    all_to_all x0 -> x2, blocking collectives: none -> 26 us  [send(): lax.all_to_all(copies, 'dp', 0, 0, axis_index_groups=groups, tiled=True)]
    all_to_all x3 -> x1, starting transfers between devices: 31 us -> 16.5 us  [send(): lax.all_to_all(copies, 'dp', 0, 0, axis_index_groups=groups, tiled=True)]
    all_to_all x3 -> x1, waiting for transfers between devices: 13.8 us -> 3.98 us  [send(): lax.all_to_all(copies, 'dp', 0, 0, axis_index_groups=groups, tiled=True)]
    dot_general x6 -> x0, matrix products: 3.76 us -> none  [the longest x2 3.16 us: document_sums(): sums = jnp.dot(grad_block.T, spread, preferred_element_type=f32)]
    ppermute x1, waiting for transfers between devices: 0.01 us -> 2.07 us  [from_neighbour(): return lax.ppermute(value, 'dp', pairs)]
    broadcast_in_dim x5 -> x1, local copies, waits for them, and re-layouts: 3.63 us -> 2.01 us  [spread(): return jnp.broadcast_to(value[None], (members, *value.shape))]
    ppermute x2, starting transfers between devices: 9.53 us -> 10.9 us  [swap_cores(): return lax.ppermute(value, 'dp', [(i, i ^ 1) for i in range(count)])]
    ppermute x1, starting transfers between devices: 3.09 us -> 2.03 us  [from_neighbour(): return lax.ppermute(value, 'dp', pairs)]
  transfers between devices with their start and end apart: 6 -> 4, of which waited for: 3 -> 4; matrix products, arithmetic and copies ran while one was open for 10% -> 2% of each run, Pallas kernels for 0% -> 0%
where the time goes in v3:
time: 94.3 us; the launch traced here: 93.9 us
  blocking collectives  43.3 us (46%)
  starting transfers between devices  29.4 us (31%)
  waiting for transfers between devices  7.85 us (8%)
  Pallas kernels  6.59 us (7%)
  local copies, waits for them, and re-layouts  4.43 us (5%)
  matrix products  1.38 us (1%)
    all_to_all x2, blocking collectives, send(): lax.all_to_all(copies, 'dp', 0, 0, axis_index_groups=groups, tiled=True)  26 us
    psum x1, blocking collectives, local(): own = lax.psum(parts, 'query').astype(bf16)  17.3 us
    all_to_all x1, starting transfers between devices, send(): lax.all_to_all(copies, 'dp', 0, 0, axis_index_groups=groups, tiled=True)  16.5 us
    ppermute x2, starting transfers between devices, swap_cores(): return lax.ppermute(value, 'dp', [(i, i ^ 1) for i in range(count)])  10.9 us
    pallas_call x1, Pallas kernels, scores_of(): pl.pallas_call(lambda *refs: finish(1.0 / token_count, slots, *refs), out...  6.23 us
    all_to_all x1, waiting for transfers between devices, send(): lax.all_to_all(copies, 'dp', 0, 0, axis_index_groups=groups, tiled=True)  3.98 us
    unnamed x14, local copies, waits for them, and re-layouts  2.43 us
    ppermute x1, waiting for transfers between devices, from_neighbour(): return lax.ppermute(value, 'dp', pairs)  2.07 us
  transfers between devices with their start and end apart: 4, of which 4 were waited for; matrix products, arithmetic and copies ran while one was open for 2% of the time, Pallas kernels for 0%

profile of v3, /device:TPU:1, one launch (start us, length us, event | category | flops | bytes accessed | tf_op | source)
XLA Modules:
  0.0 93.9 jit_solution(7217133653711479866)
XLA Ops:
  0.0 0.0 copy-start
  0.0 0.0 copy-start.6
  0.0 0.0 copy-start.4
  0.0 2.0 %broadcast_in_dim.10 = bf16[32,32,512]{2,1,0:T(8,128)(2,1)} broadcast(bf16[32,512]{1,0:T(8,128)(2,1)} %param.11), dimensions={1,2} | broadcast | bytes 1081344 | tf_op jit(solution)/shard_map/broadcast_in_dim | solution.py:268
  2.0 16.5 %all-to-all-start = ((bf16[32,32,512]{2,1,0:T(8,128)(2,1)}), bf16[32,32,512]{2,1,0:T(8,128)(2,1)S(1)}, u32[]{:S(2)}, u32[]{:S(2)}) async-start(bf16[32,32,512]{2,1,0:T(8,128)(2,1)} %broadcast_in_dim.10), calls=%async_computation | async-start | bytes 2097152 | tf_op jit(solution)/shard_map/all_to_all | solution.py:272
  18.5 0.0 copy-done.6
  18.6 0.0 copy-start.3
  18.6 0.0 copy-start.5
  18.6 0.0 copy-done
  18.6 0.0 copy-done.4
  18.6 0.7 fusion.1
  19.3 0.8 copy-done.3
  20.2 0.0 copy-done.5
  20.2 0.7 fusion.2
  20.9 0.1 select_maximum_fusion
  21.0 17.3 %all-reduce.2.own_ref.refs_1_ = bf16[528,128]{1,0:T(8,128)(2,1)S(1)} all-reduce(f32[528,128]{1,0:T(8,128)S(1)} %select_maximum_fusion), channel_id=1, replica_groups=mesh['dp'=128,'query'=4] {'query'}, use_global_device_ids=true, to_apply=%region_0.1 | all-reduce | flops 67584 | bytes 405504 | tf_op jit(solution)/shard_map/psum | solution.py:317
  38.3 5.6 %collective-permute-start = (bf16[528,128]{1,0:T(8,128)(2,1)S(1)}, bf16[528,128]{1,0:T(8,128)(2,1)S(1)}, u32[]{:S(2)}, u32[]{:S(2)}) collective-permute-start(bf16[528,128]{1,0:T(8,128)(2,1)S(1)} %all-reduce.2.own_ref.refs_1_), channel_id=1, source_target_pairs={{0,4},{4,0},{8,12},{12,8},{16,20},{20,16},{24,28},{28,24},{32,36},... | collective-permute-start | bytes 405512 | tf_op jit(solution)/shard_map/ppermute | solution.py:303
  43.9 1.0 %collective-permute-done.peer_ref.refs_2_ = bf16[528,128]{1,0:T(8,128)(2,1)S(1)} collective-permute-done((bf16[528,128]{1,0:T(8,128)(2,1)S(1)}, bf16[528,128]{1,0:T(8,128)(2,1)S(1)}, u32[]{:S(2)}, u32[]{:S(2)}) %collective-permute-start) | collective-permute-done | bytes 135200 | tf_op jit(solution)/shard_map/ppermute | solution.py:303
  44.9 0.3 grams.1
  45.2 0.0 copy-start.1
  45.2 0.7 copy-done.1
  45.9 4.0 %all-to-all-done = bf16[32,32,512]{2,1,0:T(8,128)(2,1)S(1)} async-done(((bf16[32,32,512]{2,1,0:T(8,128)(2,1)}), bf16[32,32,512]{2,1,0:T(8,128)(2,1)S(1)}, u32[]{:S(2)}, u32[]{:S(2)}) %all-to-all-start) | async-done | bytes 1048608 | tf_op jit(solution)/shard_map/all_to_all | solution.py:272
  49.9 13.3 %all_to_all.15.pieces_ref = f32[8,48,128]{2,1,0:T(8,128)S(1)} all-to-all(f32[8,48,128]{2,1,0:T(8,128)S(1)} %grams.1), channel_id=1, replica_groups={{0,8,16,24,32,40,48,56},{4,12,20,28,36,44,52,60},{64,72,80,88,96,104,11..., dimensions={0} | all-to-all | bytes 393216 | tf_op jit(solution)/shard_map/all_to_all | solution.py:272
  63.2 2.0 %collective-permute-start.1 = (bf16[32,32,512]{2,1,0:T(8,128)(2,1)S(1)}, bf16[32,32,512]{2,1,0:T(8,128)(2,1)S(1)}, u32[]{:S(2)}, u32[]{:S(2)}) collective-permute-start(bf16[32,32,512]{2,1,0:T(8,128)(2,1)S(1)} %all-to-all-done), channel_id=1, source_target_pairs={{8,0},{60,4},{16,8},{4,12},{24,16},{12,20},{32,24},{20,28},{40,32}... | collective-permute-start | bytes 3145736 | tf_op jit(solution)/shard_map/ppermute | solution.py:298
  65.3 12.6 %all_to_all.16.refs_0_ = f32[8,48,128]{2,1,0:T(8,128)S(1)} all-to-all(f32[8,48,128]{2,1,0:T(8,128)S(1)} %between.1), channel_id=1, replica_groups={{0,64,128,192,256,320,384,448},{4,68,132,196,260,324,388,452},{8,72,136..., dimensions={0} | all-to-all | bytes 393216 | tf_op jit(solution)/shard_map/all_to_all | solution.py:272
  77.9 2.1 %collective-permute-done.1 = bf16[32,32,512]{2,1,0:T(8,128)(2,1)S(1)} collective-permute-done((bf16[32,32,512]{2,1,0:T(8,128)(2,1)S(1)}, bf16[32,32,512]{2,1,0:T(8,128)(2,1)S(1)}, u32[]{:S(2)}, u32[]{:S(2)}) %collective-permute-start.1) | collective-permute-done | bytes 1048608 | tf_op jit(solution)/shard_map/ppermute | solution.py:298
  80.0 0.0 copy-start.2
  80.0 0.9 copy-done.2
  80.9 6.2 %finish.1 = (f32[16,512]{1,0:T(8,128)S(1)}, f32[16,512]{1,0:T(8,128)S(1)}) custom-call(f32[8,48,128]{2,1,0:T(8,128)S(1)} %all_to_all.16.refs_0_, bf16[528,128]{1,0:T(8,128)(2,1)S(1)} %all-reduce.2.own_ref.refs_1_, bf16[528,128]{1,0:T(8,128)(2,1)S(1)} %copy-done.2, bf16[4,8,32,512]{3,2,1,0:T(8,128)(2,1)S(1)} %bitcast.6, bf16[4,8,32,512]{3,2,1,0:T(8,128)(2,1)S(1)} %bitcast.7), custom_call_target="tpu_custom_call" | custom-call | flops 67108864 | bytes 2097152 | tf_op jit(solution)/shard_map/finish/pallas_call | solution.py:233
  87.1 5.3 %collective-permute-start.2 = (f32[16,512]{1,0:T(8,128)S(1)}, f32[16,512]{1,0:T(8,128)S(1)}, u32[]{:S(2)}, u32[]{:S(2)}) collective-permute-start(f32[16,512]{1,0:T(8,128)S(1)} %get-tuple-element.16), channel_id=1, source_target_pairs={{0,4},{4,0},{8,12},{12,8},{16,20},{20,16},{24,28},{28,24},{32,36},... | collective-permute-start | bytes 98312 | tf_op jit(solution)/shard_map/ppermute | solution.py:303
  92.4 0.8 collective-permute-done.2
  93.2 0.6 add.7
  (2 shorter events, 0.0 us)
Async XLA Ops:
  0.0 18.6 %copy-start = (bf16[512,2048]{1,0:T(8,128)(2,1)S(1)}, bf16[512,2048]{1,0:T(8,128)(2,1)}, u32[]{:S(2)}) copy-start(bf16[512,2048]{1,0:T(8,128)(2,1)} %param.6) | copy-start | bytes 6291460
  0.0 18.5 %copy-start.6 = (s32[1,16]{1,0:T(1,128)S(1)}, s32[1,16]{1,0:T(1,128)}, u32[]{:S(2)}) copy-start(s32[1,16]{1,0:T(1,128)} %param.10) | copy-start | bytes 196
  0.0 18.6 %copy-start.4 = (bf16[2048,64]{0,1:T(8,128)(2,1)S(1)}, bf16[2048,64]{0,1:T(8,128)(2,1)}, u32[]{:S(2)}) copy-start(bf16[2048,64]{0,1:T(8,128)(2,1)} %param.8) | copy-start | bytes 786436
  2.0 47.8 %all-to-all-start = ((bf16[32,32,512]{2,1,0:T(8,128)(2,1)}), bf16[32,32,512]{2,1,0:T(8,128)(2,1)S(1)}, u32[]{:S(2)}, u32[]{:S(2)}) async-start(bf16[32,32,512]{2,1,0:T(8,128)(2,1)} %broadcast_in_dim.10), calls=%async_computation | async-start | bytes 2097152 | tf_op jit(solution)/shard_map/all_to_all | solution.py:272
  18.6 1.6 %copy-start.3 = (bf16[512,2048]{1,0:T(8,128)(2,1)S(1)}, bf16[512,2048]{1,0:T(8,128)(2,1)}, u32[]{:S(2)}) copy-start(bf16[512,2048]{1,0:T(8,128)(2,1)} %param.7) | copy-start | bytes 6291460
  18.6 1.6 %copy-start.5 = (bf16[2048,64]{0,1:T(8,128)(2,1)S(1)}, bf16[2048,64]{0,1:T(8,128)(2,1)}, u32[]{:S(2)}) copy-start(bf16[2048,64]{0,1:T(8,128)(2,1)} %param.9) | copy-start | bytes 786436
  38.3 6.6 %collective-permute-start = (bf16[528,128]{1,0:T(8,128)(2,1)S(1)}, bf16[528,128]{1,0:T(8,128)(2,1)S(1)}, u32[]{:S(2)}, u32[]{:S(2)}) collective-permute-start(bf16[528,128]{1,0:T(8,128)(2,1)S(1)} %all-reduce.2.own_ref.refs_1_), channel_id=1, source_target_pairs={{0,4},{4,0},{8,12},{12,8},{16,20},{20,16},{24,28},{28,24},{32,36},... | collective-permute-start | bytes 405512 | tf_op jit(solution)/shard_map/ppermute | solution.py:303
  45.2 0.7 copy-start.1
  63.2 16.8 %collective-permute-start.1 = (bf16[32,32,512]{2,1,0:T(8,128)(2,1)S(1)}, bf16[32,32,512]{2,1,0:T(8,128)(2,1)S(1)}, u32[]{:S(2)}, u32[]{:S(2)}) collective-permute-start(bf16[32,32,512]{2,1,0:T(8,128)(2,1)S(1)} %all-to-all-done), channel_id=1, source_target_pairs={{8,0},{60,4},{16,8},{4,12},{24,16},{12,20},{32,24},{20,28},{40,32}... | collective-permute-start | bytes 3145736 | tf_op jit(solution)/shard_map/ppermute | solution.py:298
  80.0 0.9 copy-start.2
  87.1 6.1 %collective-permute-start.2 = (f32[16,512]{1,0:T(8,128)S(1)}, f32[16,512]{1,0:T(8,128)S(1)}, u32[]{:S(2)}, u32[]{:S(2)}) collective-permute-start(f32[16,512]{1,0:T(8,128)S(1)} %get-tuple-element.16), channel_id=1, source_target_pairs={{0,4},{4,0},{8,12},{12,8},{16,20},{20,16},{24,28},{28,24},{32,36},... | collective-permute-start | bytes 98312 | tf_op jit(solution)/shard_map/ppermute | solution.py:303

commit v4 on v3

--- a/solution.py
+++ b/solution.py
@@ -143,13 +143,12 @@
     return jnp.concatenate(means, axis=1)
 
 
-def finish(token_share, slots, pieces_ref, own_hbm, peer_hbm, near_hbm, far_hbm, mine_ref, other_ref, held, tokens_held, by_row, arrived, tokens_arrived):
-    tokens_copies = [
-        pltpu.make_async_copy(hbm, tokens_held.at[s], tokens_arrived.at[s])
-        for s, hbm in enumerate((own_hbm, peer_hbm))
-    ]
-    for copy in tokens_copies:
-        copy.start()
+def write_document_means(slots, own_ref, peer_ref, means_ref):
+    for s, ref in enumerate((own_ref, peer_ref)):
+        means_ref[s] = document_means(ref[...], slots)
+
+
+def finish(token_share, slots, pieces_ref, means_ref, near_hbm, far_hbm, mine_ref, other_ref, held, by_row, arrived):
     steps = held.shape[1]
     copies = [
         [
@@ -164,18 +163,14 @@
     me = lax.axis_index("dp")
     core = lax.rem(me, CORES)
     parity = lax.rem(lax.div(me, CORES), 2)
-    means = []
-    for s in range(CORES):
-        tokens_copies[s].wait()
-        means.append(document_means(tokens_held[s], slots))
     inverses = damped_inverses(unfolded(summed(pieces_ref)) * token_share)
     n = inverses.shape[0] // 2
     half = n // CORES
     fit = 2 * n // half
     docs = CORES * slots
     left = [
-        jnp.dot(inverses[n:, n:], side, precision=highest, preferred_element_type=f32)
-        for side in means
+        jnp.dot(inverses[n:, n:], means_ref[s], precision=highest, preferred_element_type=f32)
+        for s in range(CORES)
     ]
     inverse_input = inverses[:n]
     column = lax.broadcasted_iota(jnp.int32, (n, 2 * n), 1)
@@ -204,7 +199,7 @@
                 block = None
                 for j in range(fit):
                     k = first + j
-                    a = (2 * t + k // 4) * RING + 2 * (k % 4) + odd
+                    a = k * RING + 2 * t + odd
                     rows = by_row[pl.ds(pl.multiple_of(a * docs, docs), docs), :]
                     if j == 0:
                         block = rows
@@ -222,8 +217,8 @@
     other_ref[...] = total[docs // CORES :]
 
 
-def scores_of(pieces, own, peer, near, far, slots, token_count):
-    rank = own.shape[1] // 2
+def scores_of(pieces, doc_means, near, far, slots, token_count):
+    rank = doc_means.shape[1]
     docs = CORES * slots
     columns = near.shape[-1]
     vmem = pl.BlockSpec(memory_space=pltpu.VMEM)
@@ -233,14 +228,12 @@
     return pl.pallas_call(
         lambda *refs: finish(1.0 / token_count, slots, *refs),
         out_shape=(out, out),
-        in_specs=[vmem, hbm, hbm, hbm, hbm],
+        in_specs=[vmem, vmem, hbm, hbm],
         out_specs=(vmem, vmem),
         scratch_shapes=[
             pltpu.VMEM((2, *shape), bf16),
-            pltpu.VMEM((CORES, *own.shape), bf16),
             pltpu.VMEM((rank * docs, 2 * rank), f32),
             pltpu.SemaphoreType.DMA((2, shape[0])),
-            pltpu.SemaphoreType.DMA((CORES,)),
         ],
         compiler_params=pltpu.CompilerParams(vmem_limit_bytes=32 * 1024 * 1024),
         cost_estimate=pl.CostEstimate(
@@ -249,7 +242,7 @@
             transcendentals=0,
         ),
         name="finish",
-    )(pieces, own, peer, near.reshape(shape), far.reshape(shape))
+    )(pieces, doc_means, near.reshape(shape), far.reshape(shape))
 
 
 def in_vmem(kernel, out_shape, name, *operands):
@@ -282,7 +275,7 @@
 
 def every_second():
     return [
-        [place(z, y, k) for z in range(RING) for y in range(p, RING, 2)]
+        [place(z, y, k) for y in range(p, RING, 2) for z in range(RING)]
         for p in range(2)
         for k in range(CORES)
     ]
@@ -318,13 +311,20 @@
     peer = swap_cores(own)
     folded = (RING, rank * 3 // 4, 2 * rank)
     copies = in_vmem(folded_grams, folded, "grams", own, peer)
-    near, copies = lax.optimization_barrier((near, copies))
+    doc_means = in_vmem(
+        lambda *refs: write_document_means(slots, *refs),
+        (CORES, rank, slots * rank),
+        "documents",
+        own,
+        peer,
+    )
+    near, doc_means, copies = lax.optimization_barrier((near, doc_means, copies))
     copies = in_vmem(sum_and_copy, folded, "between", send(copies, along_y()))
     near, copies = lax.optimization_barrier((near, copies))
     far = from_neighbour(near)
     pieces = send(copies, along_z())
     mine, other = scores_of(
-        pieces, own, peer, near, far, slots, tokens * lax.axis_size("dp")
+        pieces, doc_means, near, far, slots, tokens * lax.axis_size("dp")
     )
     return mine + swap_cores(other)
 

time: 94.3 us -> 93.1 us (0.987)
  waiting for transfers between devices: 7.85 us -> 2.9 us
  blocking collectives: 43.3 us -> 46.2 us
    all_to_all x2, blocking collectives: 26 us -> 28.9 us  [send(): lax.all_to_all(copies, 'dp', 0, 0, axis_index_groups=groups, tiled=True)]
    all_to_all x1, waiting for transfers between devices: 3.98 us -> 1.09 us  [send(): lax.all_to_all(copies, 'dp', 0, 0, axis_index_groups=groups, tiled=True)]
    ppermute x1, waiting for transfers between devices: 2.07 us -> 0.01 us  [from_neighbour(): return lax.ppermute(value, 'dp', pairs)]
    pallas_call x1, Pallas kernels: 6.23 us -> 5.17 us  [scores_of(): pl.pallas_call(lambda *refs: finish(1.0 / token_count, slots, *refs), out...]
    pallas_call x2 -> x3, Pallas kernels: 0.36 us -> 1.4 us  [in_vmem(): pl.pallas_call(kernel, out_shape=jax.ShapeDtypeStruct(out_shape, f32), in...]
  transfers between devices with their start and end apart: 4 -> 4, of which waited for: 4 -> 3; matrix products, arithmetic and copies ran while one was open for 2% -> 2% of each run, Pallas kernels for 0% -> 1%
where the time goes in v4:
time: 93.1 us; the launch traced here: 92.6 us
  blocking collectives  46.2 us (50%)
  starting transfers between devices  29.9 us (32%)
  Pallas kernels  6.57 us (7%)
  local copies, waits for them, and re-layouts  4.74 us (5%)
  waiting for transfers between devices  2.9 us (3%)
  matrix products  1.38 us (1%)
    all_to_all x2, blocking collectives, send(): lax.all_to_all(copies, 'dp', 0, 0, axis_index_groups=groups, tiled=True)  28.9 us
    psum x1, blocking collectives, local(): own = lax.psum(parts, 'query').astype(bf16)  17.3 us
    all_to_all x1, starting transfers between devices, send(): lax.all_to_all(copies, 'dp', 0, 0, axis_index_groups=groups, tiled=True)  16.5 us
    ppermute x2, starting transfers between devices, swap_cores(): return lax.ppermute(value, 'dp', [(i, i ^ 1) for i in range(count)])  10.8 us
    pallas_call x1, Pallas kernels, scores_of(): pl.pallas_call(lambda *refs: finish(1.0 / token_count, slots, *refs), out...  5.17 us
    unnamed x14, local copies, waits for them, and re-layouts  2.73 us
    ppermute x1, starting transfers between devices, from_neighbour(): return lax.ppermute(value, 'dp', pairs)  2.58 us
    broadcast_in_dim x1, local copies, waits for them, and re-layouts, spread(): return jnp.broadcast_to(value[None], (members, *value.shape))  2.01 us
  transfers between devices with their start and end apart: 4, of which 3 were waited for; matrix products, arithmetic and copies ran while one was open for 2% of the time, Pallas kernels for 1%

profile of v4, /device:TPU:1, one launch (start us, length us, event | category | flops | bytes accessed | tf_op | source)
XLA Modules:
  0.0 92.6 jit_solution(7327412027279269892)
XLA Ops:
  0.0 0.0 copy-start
  0.0 0.0 copy-start.6
  0.0 0.0 copy-start.4
  0.0 2.0 %broadcast_in_dim.10 = bf16[32,32,512]{2,1,0:T(8,128)(2,1)} broadcast(bf16[32,512]{1,0:T(8,128)(2,1)} %param.11), dimensions={1,2} | broadcast | bytes 1081344 | tf_op jit(solution)/shard_map/broadcast_in_dim | solution.py:261
  2.0 16.5 %all-to-all-start = ((bf16[32,32,512]{2,1,0:T(8,128)(2,1)}), bf16[32,32,512]{2,1,0:T(8,128)(2,1)S(1)}, u32[]{:S(2)}, u32[]{:S(2)}) async-start(bf16[32,32,512]{2,1,0:T(8,128)(2,1)} %broadcast_in_dim.10), calls=%async_computation | async-start | bytes 2097152 | tf_op jit(solution)/shard_map/all_to_all | solution.py:265
  18.5 0.0 copy-done.6
  18.6 0.0 copy-start.3
  18.6 0.0 copy-start.5
  18.6 0.0 copy-done
  18.6 0.0 copy-done.4
  18.6 0.7 fusion.1
  19.3 0.8 copy-done.3
  20.2 0.0 copy-done.5
  20.2 0.7 fusion.2
  20.9 0.1 select_maximum_fusion
  21.0 17.3 %all-reduce.2.refs_0_.own_ref = bf16[528,128]{1,0:T(8,128)(2,1)S(1)} all-reduce(f32[528,128]{1,0:T(8,128)S(1)} %select_maximum_fusion), channel_id=1, replica_groups=mesh['dp'=128,'query'=4] {'query'}, use_global_device_ids=true, to_apply=%region_0.1 | all-reduce | flops 67584 | bytes 405504 | tf_op jit(solution)/shard_map/psum | solution.py:310
  38.3 5.6 %collective-permute-start = (bf16[528,128]{1,0:T(8,128)(2,1)S(1)}, bf16[528,128]{1,0:T(8,128)(2,1)S(1)}, u32[]{:S(2)}, u32[]{:S(2)}) collective-permute-start(bf16[528,128]{1,0:T(8,128)(2,1)S(1)} %all-reduce.2.refs_0_.own_ref), channel_id=1, source_target_pairs={{0,4},{4,0},{8,12},{12,8},{16,20},{20,16},{24,28},{28,24},{32,36},... | collective-permute-start | bytes 405512 | tf_op jit(solution)/shard_map/ppermute | solution.py:296
  43.9 1.0 %collective-permute-done.refs_1_.peer_ref = bf16[528,128]{1,0:T(8,128)(2,1)S(1)} collective-permute-done((bf16[528,128]{1,0:T(8,128)(2,1)S(1)}, bf16[528,128]{1,0:T(8,128)(2,1)S(1)}, u32[]{:S(2)}, u32[]{:S(2)}) %collective-permute-start) | collective-permute-done | bytes 135200 | tf_op jit(solution)/shard_map/ppermute | solution.py:296
  44.9 0.3 grams.1
  45.2 1.0 %documents.1.refs_1_ = f32[2,64,1024]{2,1,0:T(8,128)S(1)} custom-call(bf16[528,128]{1,0:T(8,128)(2,1)S(1)} %all-reduce.2.refs_0_.own_ref, bf16[528,128]{1,0:T(8,128)(2,1)S(1)} %collective-permute-done.refs_1_.peer_ref), custom_call_target="tpu_custom_call" | custom-call | tf_op jit(solution)/shard_map/documents/pallas_call | solution.py:250
  46.3 0.0 copy-start.1
  46.3 0.8 copy-done.1
  47.1 1.1 %all-to-all-done = bf16[32,32,512]{2,1,0:T(8,128)(2,1)S(1)} async-done(((bf16[32,32,512]{2,1,0:T(8,128)(2,1)}), bf16[32,32,512]{2,1,0:T(8,128)(2,1)S(1)}, u32[]{:S(2)}, u32[]{:S(2)}) %all-to-all-start) | async-done | bytes 1048608 | tf_op jit(solution)/shard_map/all_to_all | solution.py:265
  48.2 13.7 %all_to_all.15.pieces_ref = f32[8,48,128]{2,1,0:T(8,128)S(1)} all-to-all(f32[8,48,128]{2,1,0:T(8,128)S(1)} %grams.1), channel_id=1, replica_groups={{0,8,16,24,32,40,48,56},{4,12,20,28,36,44,52,60},{64,72,80,88,96,104,11..., dimensions={0} | all-to-all | bytes 393216 | tf_op jit(solution)/shard_map/all_to_all | solution.py:265
  61.9 2.6 %collective-permute-start.1 = (bf16[32,32,512]{2,1,0:T(8,128)(2,1)S(1)}, bf16[32,32,512]{2,1,0:T(8,128)(2,1)S(1)}, u32[]{:S(2)}, u32[]{:S(2)}) collective-permute-start(bf16[32,32,512]{2,1,0:T(8,128)(2,1)S(1)} %all-to-all-done), channel_id=1, source_target_pairs={{8,0},{60,4},{16,8},{4,12},{24,16},{12,20},{32,24},{20,28},{40,32}... | collective-permute-start | bytes 3145736 | tf_op jit(solution)/shard_map/ppermute | solution.py:291
  64.5 15.3 %all_to_all.16.refs_0_ = f32[8,48,128]{2,1,0:T(8,128)S(1)} all-to-all(f32[8,48,128]{2,1,0:T(8,128)S(1)} %between.1), channel_id=1, replica_groups={{0,64,128,192,256,320,384,448},{4,68,132,196,260,324,388,452},{8,72,136..., dimensions={0} | all-to-all | bytes 393216 | tf_op jit(solution)/shard_map/all_to_all | solution.py:265
  79.8 0.0 collective-permute-done.1
  79.8 1.0 %copy-done.2 = f32[2,64,1024]{2,1,0:T(8,128)S(1)} copy-done((f32[2,64,1024]{2,1,0:T(8,128)S(1)}, f32[2,64,1024]{2,1,0:T(8,128)}, u32[]{:S(2)}) %copy-start.2) | copy-done | bytes 524312
  80.8 5.2 %finish.1 = (f32[16,512]{1,0:T(8,128)S(1)}, f32[16,512]{1,0:T(8,128)S(1)}) custom-call(f32[8,48,128]{2,1,0:T(8,128)S(1)} %all_to_all.16.refs_0_, f32[2,64,1024]{2,1,0:T(8,128)S(1)} %copy-done.2, bf16[4,8,32,512]{3,2,1,0:T(8,128)(2,1)S(1)} %bitcast.6, bf16[4,8,32,512]{3,2,1,0:T(8,128)(2,1)S(1)} %bitcast.7), custom_call_target="tpu_custom_call" | custom-call | flops 67108864 | bytes 2097152 | tf_op jit(solution)/shard_map/finish/pallas_call | solution.py:228
  86.0 5.2 %collective-permute-start.2 = (f32[16,512]{1,0:T(8,128)S(1)}, f32[16,512]{1,0:T(8,128)S(1)}, u32[]{:S(2)}, u32[]{:S(2)}) collective-permute-start(f32[16,512]{1,0:T(8,128)S(1)} %get-tuple-element.18), channel_id=1, source_target_pairs={{0,4},{4,0},{8,12},{12,8},{16,20},{20,16},{24,28},{28,24},{32,36},... | collective-permute-start | bytes 98312 | tf_op jit(solution)/shard_map/ppermute | solution.py:296
  91.2 0.8 collective-permute-done.2
  92.0 0.6 add.7
  (3 shorter events, 0.0 us)
Async XLA Ops:
  0.0 18.6 %copy-start = (bf16[512,2048]{1,0:T(8,128)(2,1)S(1)}, bf16[512,2048]{1,0:T(8,128)(2,1)}, u32[]{:S(2)}) copy-start(bf16[512,2048]{1,0:T(8,128)(2,1)} %param.6) | copy-start | bytes 6291460
  0.0 18.5 %copy-start.6 = (s32[1,16]{1,0:T(1,128)S(1)}, s32[1,16]{1,0:T(1,128)}, u32[]{:S(2)}) copy-start(s32[1,16]{1,0:T(1,128)} %param.10) | copy-start | bytes 196
  0.0 18.6 %copy-start.4 = (bf16[2048,64]{0,1:T(8,128)(2,1)S(1)}, bf16[2048,64]{0,1:T(8,128)(2,1)}, u32[]{:S(2)}) copy-start(bf16[2048,64]{0,1:T(8,128)(2,1)} %param.8) | copy-start | bytes 786436
  2.0 46.2 %all-to-all-start = ((bf16[32,32,512]{2,1,0:T(8,128)(2,1)}), bf16[32,32,512]{2,1,0:T(8,128)(2,1)S(1)}, u32[]{:S(2)}, u32[]{:S(2)}) async-start(bf16[32,32,512]{2,1,0:T(8,128)(2,1)} %broadcast_in_dim.10), calls=%async_computation | async-start | bytes 2097152 | tf_op jit(solution)/shard_map/all_to_all | solution.py:265
  18.6 1.6 %copy-start.3 = (bf16[512,2048]{1,0:T(8,128)(2,1)S(1)}, bf16[512,2048]{1,0:T(8,128)(2,1)}, u32[]{:S(2)}) copy-start(bf16[512,2048]{1,0:T(8,128)(2,1)} %param.7) | copy-start | bytes 6291460
  18.6 1.6 %copy-start.5 = (bf16[2048,64]{0,1:T(8,128)(2,1)S(1)}, bf16[2048,64]{0,1:T(8,128)(2,1)}, u32[]{:S(2)}) copy-start(bf16[2048,64]{0,1:T(8,128)(2,1)} %param.9) | copy-start | bytes 786436
  38.3 6.6 %collective-permute-start = (bf16[528,128]{1,0:T(8,128)(2,1)S(1)}, bf16[528,128]{1,0:T(8,128)(2,1)S(1)}, u32[]{:S(2)}, u32[]{:S(2)}) collective-permute-start(bf16[528,128]{1,0:T(8,128)(2,1)S(1)} %all-reduce.2.refs_0_.own_ref), channel_id=1, source_target_pairs={{0,4},{4,0},{8,12},{12,8},{16,20},{20,16},{24,28},{28,24},{32,36},... | collective-permute-start | bytes 405512 | tf_op jit(solution)/shard_map/ppermute | solution.py:296
  46.3 0.8 copy-start.1
  61.9 17.9 %collective-permute-start.1 = (bf16[32,32,512]{2,1,0:T(8,128)(2,1)S(1)}, bf16[32,32,512]{2,1,0:T(8,128)(2,1)S(1)}, u32[]{:S(2)}, u32[]{:S(2)}) collective-permute-start(bf16[32,32,512]{2,1,0:T(8,128)(2,1)S(1)} %all-to-all-done), channel_id=1, source_target_pairs={{8,0},{60,4},{16,8},{4,12},{24,16},{12,20},{32,24},{20,28},{40,32}... | collective-permute-start | bytes 3145736 | tf_op jit(solution)/shard_map/ppermute | solution.py:291
  79.8 1.0 %copy-start.2 = (f32[2,64,1024]{2,1,0:T(8,128)S(1)}, f32[2,64,1024]{2,1,0:T(8,128)}, u32[]{:S(2)}) copy-start(f32[2,64,1024]{2,1,0:T(8,128)} %copy-done.1) | copy-start | bytes 1572868
  86.0 6.0 %collective-permute-start.2 = (f32[16,512]{1,0:T(8,128)S(1)}, f32[16,512]{1,0:T(8,128)S(1)}, u32[]{:S(2)}, u32[]{:S(2)}) collective-permute-start(f32[16,512]{1,0:T(8,128)S(1)} %get-tuple-element.18), channel_id=1, source_target_pairs={{0,4},{4,0},{8,12},{12,8},{16,20},{20,16},{24,28},{28,24},{32,36},... | collective-permute-start | bytes 98312 | tf_op jit(solution)/shard_map/ppermute | solution.py:296
